TPU v7x, 256 devices: a whole 4x4x8 slice. The times are simulated.
256 devices in a mesh: dp: 32 (over z, x), tensor: 8 (over y, core).
Axes of the slice: x: 4, y: 4, z: 8, core: 2. Of those that a mesh axis runs over, the one named last changes fastest.
Arguments:
- activations: bfloat16 [28672, 4096], P('dp', 'tensor'), may hold values from -6 to 6
- out_grads: bfloat16 [28672, 4096], P('dp', 'tensor'), may hold values from -6 to 6
- gate_act: bfloat16 [28672, 14336], P('dp', 'tensor'), may hold values from -6 to 6
- w_down: bfloat16 [14336, 4096], P('tensor', 'dp'), may hold values from -0.09375 to 0.09375
- proj_in: bfloat16 [4096, 64], P('tensor'), may hold values from -0.09375 to 0.09375
- proj_out: bfloat16 [14336, 64], P('tensor'), may hold values from -0.046875 to 0.046875
- lengths: int32 [32, 8], P('dp'), may hold values from 1 to 448, 896 in all within a row
- assign: int32 [256], replicated, may hold values from 0 to 255, each once
Outputs:
- loggrads: float32 [256, 64, 64], P('dp', 'tensor')
Inputs may be any that keep to these rules, and one draw needn't show every extreme that they name: `lengths`: each row gives the token counts of the 8 sequences packed into one data group's 896 rows and sums to 896. `assign`: a permutation of the sequence numbers.
All inputs are finite; a program needn't handle non-finite values.
Results may differ from a plain program's by a relative error of at most 0.013.
Values may be sent and summed in bfloat16 or wider, within the bound.
No kernel may reach another device: no remote copies, remote signals or barrier semaphores. Data moves between devices by JAX's collectives and lax.ppermute only.
A program may use at most 128 MiB of HBM per device.

v0:
```python
import jax
import jax.numpy as jnp
from jax import lax
from jax.sharding import PartitionSpec as P


def shards(activations, out_grads, gate_act, w_down, proj_in, proj_out, lengths, assign):
    tok_rows = activations.shape[0]
    rank_all = proj_in.shape[1]
    full_grads = lax.all_gather(out_grads, "tensor", axis=1, tiled=True)
    hidden_grad = lax.dot_general(
        full_grads,
        lax.all_gather(w_down, "dp", axis=1, tiled=True),
        (((1,), (1,)), ((), ())),
        preferred_element_type=jnp.float32,
    )
    up_grad = (hidden_grad * gate_act.astype(jnp.float32)).astype(jnp.bfloat16)
    out_part = jnp.dot(up_grad, proj_out, preferred_element_type=jnp.float32)
    in_part = jnp.dot(activations, proj_in, preferred_element_type=jnp.float32)
    col_count = rank_all // lax.axis_size("tensor")
    shard_index = lax.axis_index("tensor")
    in_sum, out_sum = lax.psum((in_part, out_part), "tensor")
    in_mine = lax.dynamic_slice_in_dim(in_sum, shard_index * col_count, col_count, 1)
    seq_lengths = lengths[0]
    seq_ends = jnp.cumsum(seq_lengths)
    starts = seq_ends - seq_lengths
    positions = lax.iota(jnp.int32, tok_rows)
    inside = (positions[None, :] >= starts[:, None]) & (positions[None, :] < seq_ends[:, None])
    member = jnp.where(inside, 1.0 / seq_lengths[:, None].astype(jnp.float32), 0.0)
    weighted = member[:, :, None] * in_mine[None, :, :]
    result = jnp.einsum("ctp,tq->cpq", weighted, out_sum, precision=lax.Precision.HIGHEST)
    per_group = seq_lengths.shape[0]
    group_count = lax.axis_size("dp")
    seq_total = per_group * group_count
    group_index = lax.axis_index("dp")
    mine_ids = lax.dynamic_slice_in_dim(assign, group_index * per_group, per_group, 0)
    placing = (mine_ids[None, :] == lax.iota(jnp.int32, seq_total)[:, None]).astype(jnp.float32)
    flat_result = result.reshape(per_group, col_count * rank_all)
    spread = jnp.dot(placing, flat_result, precision=lax.Precision.HIGHEST)
    owned = lax.psum_scatter(
        spread.astype(jnp.bfloat16), "dp", scatter_dimension=0, tiled=True
    ).astype(jnp.float32)
    return owned.reshape(per_group, col_count, rank_all)


def solution(mesh):
    in_specs = (
        P("dp", "tensor"),
        P("dp", "tensor"),
        P("dp", "tensor"),
        P("tensor", "dp"),
        P("tensor", None),
        P("tensor", None),
        P("dp", None),
        P(),
    )
    out_specs = P("dp", "tensor", None)
    return jax.shard_map(shards, mesh=mesh, in_specs=in_specs, out_specs=out_specs, check_vma=False)
```

profile of v0, /device:TPU:32, one launch (start us, length us, event | category | flops | bytes accessed | tf_op | source)
XLA Modules:
  0.0 510.3 jit_solution(17634856475808253684)
XLA Ops:
  6.5 0.0 copy-start
  6.5 0.0 all-gather.3.cloned.1.call-start
  6.5 0.7 all-gather.3.cloned.1.call-update
  7.3 0.0 all-gather.5.cloned.1.call-start
  7.3 0.7 all-gather.5.cloned.1.call-update
  8.0 0.0 all-reduce.3.cloned.1.call-start
  8.1 0.8 reduce-window.7
  8.9 0.7 bitcast_subtract_fusion
  9.5 0.0 copy-done
  9.5 2.0 fusion.10
  11.5 0.0 copy-start.2
  11.5 0.0 copy-start.1
  11.5 48.2 %all-gather.3.cloned.1.call-done = bf16[896,4096]{1,0:T(8,128)(2,1)} async-done(((bf16[896,512]{1,0:T(8,128)(2,1)}), bf16[896,4096]{1,0:T(8,128)(2,1)}) %all-gather.3.cloned.1.call-update) | async-done | bytes 7340048 | tf_op jit(solution)/shard_map/all_gather | solution.py:10
  59.7 141.1 %all-gather.5.cloned.1.call-done = bf16[1792,4096]{1,0:T(8,128)(2,1)} async-done(((bf16[1792,128]{1,0:T(8,128)(2,1)}), bf16[1792,4096]{1,0:T(8,128)(2,1)}) %all-gather.5.cloned.1.call-update) | async-done | bytes 14680080 | tf_op jit(solution)/shard_map/all_gather | solution.py:13
  200.8 23.2 %fusion = f32[896,64]{0,1:T(8,128)} fusion(bf16[1792,64]{0,1:T(8,128)(2,1)} %param.13, bf16[896,1792]{1,0:T(8,128)(2,1)} %param.10, bf16[896,4096]{1,0:T(8,128)(2,1)} %all-gather.3.cloned.1.call-done, bf16[1792,4096]{1,0:T(8,128)(2,1)} %all-gather.5.cloned.1.call-done), kind=kOutput, calls=%fused_computation.1 | convolution fusion | flops 13363675136 | bytes 25690112 | tf_op jit(solution)/shard_map/dot_general | solution.py:18
  224.0 0.0 all-reduce.3.cloned.1.call-update
  224.0 0.0 reduce-scatter.2.cloned.1.call-start
  224.1 0.0 copy-done.2
  224.1 0.0 copy-done.1
  224.1 0.1 dynamic_slice.6
  224.2 0.1 fusion.8
  224.3 63.0 %all-reduce.3.cloned.1.call-done = (f32[896,64]{0,1:T(8,128)}, f32[896,64]{0,1:T(8,128)}) async-done(((f32[896,64]{0,1:T(8,128)}, f32[896,64]{0,1:T(8,128)}), (f32[896,64]{0,1:T(8,128)}, f32[896,64]{0,1:T(8,128)})) %all-reduce.3.cloned.1.call-update) | async-done | bytes 458768 | tf_op jit(solution)/shard_map/psum | solution.py:22
  287.2 0.8 constant_dynamic-slice_fusion
  288.0 1.3 fusion.1
  289.3 0.1 reshape.108
  289.4 1.0 convolution_convert_fusion
  290.4 0.0 reduce-scatter.2.cloned.1.call-update
  290.4 211.9 %reduce-scatter.2.cloned.1.call-done = bf16[8,512]{1,0:T(8,128)(2,1)} async-done(((bf16[256,512]{1,0:T(8,128)(2,1)}), bf16[8,512]{1,0:T(8,128)(2,1)}) %reduce-scatter.2.cloned.1.call-update) | async-done | bytes 8208 | tf_op jit(solution)/shard_map/reduce_scatter | solution.py:40
  502.3 1.4 reshape.112
  (1 shorter events, 0.0 us)
Async XLA Ops:
  6.5 3.0 copy-start
  6.5 53.2 %all-gather.3.cloned.1.call-start = ((), (), s32[]{:S(2)}) async-start(), calls=%async_computation.1 | async-start | bytes 8257536 | tf_op jit(solution)/shard_map/all_gather | solution.py:10
  7.3 193.5 %all-gather.5.cloned.1.call-start = ((), (), s32[]{:S(2)}) async-start(), calls=%async_computation.2 | async-start | bytes 15138816 | tf_op jit(solution)/shard_map/all_gather | solution.py:13
  8.0 279.2 %all-reduce.3.cloned.1.call-start = ((), (), s32[]{:S(2)}) async-start(), calls=%async_computation.4 | async-start | bytes 917504 | tf_op jit(solution)/shard_map/psum | solution.py:22
  11.5 212.6 %copy-start.2 = (s32[1,8]{1,0:T(1,128)S(1)}, s32[1,8]{1,0:T(1,128)}, u32[]{:S(2)}) copy-start(s32[1,8]{1,0:T(1,128)} %param.14) | copy-start | bytes 100
  11.5 212.6 %copy-start.1 = (s32[256]{0:T(256)S(1)}, s32[256]{0:T(256)}, u32[]{:S(2)}) copy-start(s32[256]{0:T(256)} %param.15) | copy-start | bytes 3076
  224.0 278.3 %reduce-scatter.2.cloned.1.call-start = ((), (), s32[]{:S(2)}) async-start(), calls=%async_computation.3 | async-start | bytes 270336 | tf_op jit(solution)/shard_map/reduce_scatter | solution.py:40
Sparse Core Ops, SparseCore 0:
  9.2 50.4 all-gather.2
  62.2 138.5 all-gather.4
  224.2 63.0 all-reduce.2
  291.4 210.9 reduce-scatter.1
where the time goes:
time: 512 us; the launch traced here: 510 us
  waiting for transfers between devices  466 us (91%)
  matrix products  27.5 us (5%)
  between operations  13.2 us (3%)
    reduce_scatter x1, waiting for transfers between devices, shards(): lax.psum_scatter(spread.astype(jnp.bfloat16), 'dp', scatter_dimension=0,...  212 us
    all_gather x1, waiting for transfers between devices, shards(): lax.all_gather(w_down, 'dp', axis=1, tiled=True)  141 us
    psum x1, waiting for transfers between devices, shards(): in_sum, out_sum = lax.psum((in_part, out_part), 'tensor')  63 us
    all_gather x1, waiting for transfers between devices, shards(): full_grads = lax.all_gather(out_grads, 'tensor', axis=1, tiled=True)  48.2 us
    dot_general x1, matrix products, shards(): out_part = jnp.dot(up_grad, proj_out, preferred_element_type=jnp.float32)  23.2 us
  transfers between devices with their start and end apart: 4, of which 4 were waited for; matrix products, arithmetic and copies ran while one was open for 1% of the time, Pallas kernels for 0%

commit v1 on v0

v1 whole, which is shorter than its diff:
```python
import jax
import jax.numpy as jnp
from jax import lax
from jax.sharding import PartitionSpec as P


def member_of(seq_lengths, tok_rows):
    slots = seq_lengths.shape[0]
    before = lax.iota(jnp.int32, slots)[None, :] < lax.iota(jnp.int32, slots)[:, None]
    starts = jnp.sum(jnp.where(before, seq_lengths[None, :], 0), axis=1)
    ends = starts + seq_lengths
    positions = lax.iota(jnp.int32, tok_rows)
    inside = (positions[None, :] >= starts[:, None]) & (positions[None, :] < ends[:, None])
    return jnp.where(inside, 1.0 / seq_lengths[:, None].astype(jnp.float32), 0.0)


def place(result, assign):
    slots, values = result.shape
    groups = lax.axis_size("dp")
    mine = lax.dynamic_slice_in_dim(assign, lax.axis_index("dp") * slots, slots, 0)
    placing = (mine[None, :] == lax.iota(jnp.int32, slots * groups)[:, None]).astype(jnp.bfloat16)
    spread = jnp.dot(placing, result, preferred_element_type=jnp.float32).astype(jnp.bfloat16)
    got = lax.all_to_all(spread, "dp", split_axis=0, concat_axis=0, tiled=True)
    return jnp.sum(got.reshape(groups, slots, values).astype(jnp.float32), axis=0)


def shards(activations, out_grads, gate_act, w_down, proj_in, proj_out, lengths, assign):
    tok_rows = activations.shape[0]
    rank_all = proj_in.shape[1]
    shard_count = lax.axis_size("tensor")
    slots = lengths.shape[1]
    cols = rank_all // shard_count

    in_part = jnp.dot(activations, proj_in, preferred_element_type=jnp.float32)
    in_high = in_part.astype(jnp.bfloat16)
    in_low = (in_part - in_high.astype(jnp.float32)).astype(jnp.bfloat16)
    full_grads = lax.all_gather(out_grads, "tensor", axis=1, tiled=True)
    in_all = lax.all_gather(jnp.concatenate([in_high, in_low], axis=1), "tensor", axis=0)
    in_all = jnp.sum(in_all.astype(jnp.float32), axis=0)
    in_sum = in_all[:, :rank_all] + in_all[:, rank_all:]
    weighted = member_of(lengths[0], tok_rows)[:, :, None] * in_sum[None, :, :]

    hidden_grad = lax.dot_general(
        full_grads,
        lax.all_gather(w_down, "dp", axis=1, tiled=True),
        (((1,), (1,)), ((), ())),
        preferred_element_type=jnp.float32,
    )
    up_grad = (hidden_grad * gate_act.astype(jnp.float32)).astype(jnp.bfloat16)
    out_part = jnp.dot(up_grad, proj_out, preferred_element_type=jnp.float32)
    part = jnp.einsum("ctp,tq->cpq", weighted, out_part, precision=lax.Precision.HIGHEST)
    part = part.reshape(slots, shard_count, cols * rank_all).transpose(1, 0, 2)
    result = jnp.sum(lax.all_to_all(part, "tensor", split_axis=0, concat_axis=0, tiled=True), axis=0)
    return place(result.astype(jnp.bfloat16), assign).reshape(slots, cols, rank_all)


def solution(mesh):
    in_specs = (
        P("dp", "tensor"),
        P("dp", "tensor"),
        P("dp", "tensor"),
        P("tensor", "dp"),
        P("tensor", None),
        P("tensor", None),
        P("dp", None),
        P(),
    )
    out_specs = P("dp", "tensor", None)
    return jax.shard_map(shards, mesh=mesh, in_specs=in_specs, out_specs=out_specs, check_vma=False)
```

time: 512 us -> 291 us (0.57)
  waiting for transfers between devices: 466 us -> 222 us
  blocking collectives: 0 us -> 17.7 us
    reduce_scatter x1 -> x0, waiting for transfers between devices: 212 us -> none  [shards(): lax.psum_scatter(spread.astype(jnp.bfloat16), 'dp', scatter_dimension=0,...]
    psum x1 -> x0, waiting for transfers between devices: 63 us -> none  [shards(): in_sum, out_sum = lax.psum((in_part, out_part), 'tensor')]
    all_gather x0 -> x1, waiting for transfers between devices: none -> 26.7 us  [shards(): lax.all_gather(jnp.concatenate([in_high, in_low], axis=1), 'tensor', axis=0)]
    all_to_all x0 -> x1, blocking collectives: none -> 17.7 us  [place(): got = lax.all_to_all(spread, 'dp', split_axis=0, concat_axis=0, tiled=True)]
    all_to_all x0 -> x1, waiting for transfers between devices: none -> 6.05 us  [shards(): lax.all_to_all(part, 'tensor', split_axis=0, concat_axis=0, tiled=True)]
  transfers between devices with their start and end apart: 4 -> 4, of which waited for: 4 -> 4; matrix products, arithmetic and copies ran while one was open for 1% -> 2% of each run, Pallas kernels for 0% -> 0%
where the time goes in v1:
time: 291 us
  waiting for transfers between devices  222 us (76%)
  matrix products  25.2 us (9%)
  blocking collectives  17.7 us (6%)
  between operations  13.2 us (5%)
  other arithmetic  5.72 us (2%)
  starting transfers between devices  4.37 us (2%)
  local copies, waits for them, and re-layouts  3.43 us (1%)
    all_gather x1, waiting for transfers between devices, shards(): lax.all_gather(w_down, 'dp', axis=1, tiled=True)  141 us
    all_gather x1, waiting for transfers between devices, shards(): full_grads = lax.all_gather(out_grads, 'tensor', axis=1, tiled=True)  46.3 us
    all_gather x1, waiting for transfers between devices, shards(): lax.all_gather(jnp.concatenate([in_high, in_low], axis=1), 'tensor', axis=0)  26.7 us
    dot_general x1, matrix products, shards(): out_part = jnp.dot(up_grad, proj_out, preferred_element_type=jnp.float32)  22 us
    all_to_all x1, blocking collectives, place(): got = lax.all_to_all(spread, 'dp', split_axis=0, concat_axis=0, tiled=True)  17.7 us
    all_to_all x1, waiting for transfers between devices, shards(): lax.all_to_all(part, 'tensor', split_axis=0, concat_axis=0, tiled=True)  6.05 us
  transfers between devices with their start and end apart: 4, of which 4 were waited for; matrix products, arithmetic and copies ran while one was open for 2% of the time, Pallas kernels for 0%

profile of v1, /device:TPU:32, one launch (start us, length us, event | category | flops | bytes accessed | tf_op | source)
XLA Modules:
  0.0 291.1 jit_solution(1241002359419916471)
XLA Ops:
  6.5 0.0 copy-start
  6.5 0.0 all-gather.9.cloned.1.call-start
  6.5 1.2 copy-done
  7.7 1.3 subtract_convert_fusion
  9.0 0.7 pad_maximum_fusion
  9.7 0.0 all-gather.9.cloned.1.call-update
  9.7 0.0 all-gather.5.cloned.1.call-start
  9.8 0.7 all-gather.5.cloned.1.call-update
  10.5 0.0 all-gather.7.cloned.1.call-start
  10.5 0.7 all-gather.7.cloned.1.call-update
  11.2 0.8 select_reduce_fusion
  12.0 0.7 convert_divide_fusion
  12.7 0.7 bitcast_add_fusion
  13.3 0.1 fusion.9
  13.4 26.7 %all-gather.9.cloned.1.call-done = bf16[7168,128]{0,1:T(8,128)(2,1)} async-done(((bf16[896,128]{0,1:T(8,128)(2,1)}), bf16[7168,128]{0,1:T(8,128)(2,1)}) %all-gather.9.cloned.1.call-update) | async-done | bytes 1835024 | tf_op jit(solution)/shard_map/all_gather | solution.py:38
  40.1 1.9 convert_element_type.46
  42.0 0.0 copy-start.1
  42.0 0.6 copy.11
  42.7 0.9 bitcast_reduce_fusion
  43.6 0.0 copy-start.2
  43.6 46.3 %all-gather.5.cloned.1.call-done = bf16[896,4096]{1,0:T(8,128)(2,1)} async-done(((bf16[896,512]{1,0:T(8,128)(2,1)}), bf16[896,4096]{1,0:T(8,128)(2,1)}) %all-gather.5.cloned.1.call-update) | async-done | bytes 7340048 | tf_op jit(solution)/shard_map/all_gather | solution.py:37
  89.8 141.1 %all-gather.7.cloned.1.call-done = bf16[1792,4096]{1,0:T(8,128)(2,1)} async-done(((bf16[1792,128]{1,0:T(8,128)(2,1)}), bf16[1792,4096]{1,0:T(8,128)(2,1)}) %all-gather.7.cloned.1.call-update) | async-done | bytes 14680080 | tf_op jit(solution)/shard_map/all_gather | solution.py:45
  230.9 0.0 copy-done.1
  230.9 22.0 %fusion.4 = f32[896,64,1]{0,1,2:T(8,128)S(1)} fusion(bf16[1792,64]{0,1:T(8,128)(2,1)S(1)} %copy-done.1, bf16[896,1792]{1,0:T(8,128)(2,1)} %param.10, bf16[896,4096]{1,0:T(8,128)(2,1)} %all-gather.5.cloned.1.call-done, bf16[1792,4096]{1,0:T(8,128)(2,1)} %all-gather.7.cloned.1.call-done), kind=kOutput, calls=%fused_computation.7 | convolution fusion | flops 13363675136 | bytes 25690112 | tf_op jit(solution)/shard_map/dot_general | solution.py:50
  253.0 1.7 fusion.1
  254.6 0.1 reshape.85
  254.8 0.7 copy.13
  255.5 4.3 %all-to-all-start = ((f32[8,8,512]{2,1,0:T(8,128)}), f32[8,8,512]{2,1,0:T(8,128)S(1)}, u32[]{:S(2)}, u32[]{:S(2)}) async-start(f32[8,8,512]{2,1,0:T(8,128)} %bitcast.21), calls=%async_computation | async-start | bytes 262144 | tf_op jit(solution)/shard_map/all_to_all | solution.py:53
  259.8 0.0 copy-done.2
  259.8 0.1 dynamic_slice.3
  259.8 6.1 %all-to-all-done = f32[8,8,512]{2,1,0:T(8,128)S(1)} async-done(((f32[8,8,512]{2,1,0:T(8,128)}), f32[8,8,512]{2,1,0:T(8,128)S(1)}, u32[]{:S(2)}, u32[]{:S(2)}) %all-to-all-start) | async-done | bytes 131104 | tf_op jit(solution)/shard_map/all_to_all | solution.py:53
  265.9 0.2 fusion.3
  266.1 17.7 %all_to_all.14 = bf16[32,8,512]{2,1,0:T(8,128)(2,1)S(1)} all-to-all(bf16[32,8,512]{2,1,0:T(8,128)(2,1)S(1)} %fusion.3), channel_id=1, replica_groups=mesh['dp'=32,'tensor'=8] {'dp'}, dimensions={0} | all-to-all | bytes 524288 | tf_op jit(solution)/shard_map/all_to_all | solution.py:23
  283.9 0.7 reshape.86
  (3 shorter events, 0.1 us)
Async XLA Ops:
  6.5 1.2 copy-start
  6.5 33.6 %all-gather.9.cloned.1.call-start = ((), (), s32[]{:S(2)}) async-start(), calls=%async_computation.4 | async-start | bytes 2064384 | tf_op jit(solution)/shard_map/all_gather | solution.py:38
  9.7 80.1 %all-gather.5.cloned.1.call-start = ((), (), s32[]{:S(2)}) async-start(), calls=%async_computation.2 | async-start | bytes 8257536 | tf_op jit(solution)/shard_map/all_gather | solution.py:37
  10.5 220.4 %all-gather.7.cloned.1.call-start = ((), (), s32[]{:S(2)}) async-start(), calls=%async_computation.3 | async-start | bytes 15138816 | tf_op jit(solution)/shard_map/all_gather | solution.py:45
  42.0 188.9 %copy-start.1 = (bf16[1792,64]{0,1:T(8,128)(2,1)S(1)}, bf16[1792,64]{0,1:T(8,128)(2,1)}, u32[]{:S(2)}) copy-start(bf16[1792,64]{0,1:T(8,128)(2,1)} %param.13) | copy-start | bytes 688132
  43.6 216.2 %copy-start.2 = (s32[256]{0:T(256)S(1)}, s32[256]{0:T(256)}, u32[]{:S(2)}) copy-start(s32[256]{0:T(256)} %param.15) | copy-start | bytes 3076
  255.5 10.4 %all-to-all-start = ((f32[8,8,512]{2,1,0:T(8,128)}), f32[8,8,512]{2,1,0:T(8,128)S(1)}, u32[]{:S(2)}, u32[]{:S(2)}) async-start(f32[8,8,512]{2,1,0:T(8,128)} %bitcast.21), calls=%async_computation | async-start | bytes 262144 | tf_op jit(solution)/shard_map/all_to_all | solution.py:53
Sparse Core Ops, SparseCore 0:
  9.9 30.2 all-gather.8
  42.0 47.8 all-gather.4
  92.3 138.5 all-gather.6

commit v2 on v1

v2 whole, which is shorter than its diff:
```python
import functools

import jax
import jax.numpy as jnp
from jax import lax
from jax.experimental import pallas as pl
from jax.experimental.layout import Layout, with_layout_constraint
from jax.experimental.pallas import tpu as pltpu
from jax.sharding import PartitionSpec as P

NZ, NX, NY, NC = 8, 4, 4, 2
TILE = 384
DISTANCES = (0, -1, 1, -2, 2, -3, 3, 4)
PARTS = 4
VMEM = 58 * 2**20
FIRST = 768


def move(array, axis, dist):
    if axis == "z":
        pairs = [(z * NX + x, (z + dist) % NZ * NX + x) for z in range(NZ) for x in range(NX)]
        return lax.ppermute(array, "dp", pairs)
    if axis == "x":
        pairs = [(z * NX + x, z * NX + (x + dist) % NX) for z in range(NZ) for x in range(NX)]
        return lax.ppermute(array, "dp", pairs)
    if axis == "y":
        pairs = [(y * NC + c, (y + dist) % NY * NC + c) for y in range(NY) for c in range(NC)]
        return lax.ppermute(array, "tensor", pairs)
    pairs = [(y * NC + c, y * NC + (c + dist) % NC) for y in range(NY) for c in range(NC)]
    return lax.ppermute(array, "tensor", pairs)


class Blocks:
    def __init__(self, array, stretches):
        self.array, self.stretches = array, stretches

    def sent(self, axis, dist, name):
        dz, dx = (dist, 0) if axis == "z" else (0, dist)
        with jax.named_scope(name):
            array = move(self.array, axis, dist)
        return Blocks(array, [(z - dz, x - dx, r, n) for z, x, r, n in self.stretches])

    def part(self, begin, end):
        kept, at = [], 0
        for z, x, r, n in self.stretches:
            low, high = max(begin, at), min(end, at + n)
            if low < high:
                kept.append((z, x, r + low - at, high - low))
            at += n
        return Blocks(self.array[begin:end], kept)

    def halves(self):
        rows = self.array.shape[0]
        middle = rows // 32 * 16
        return self.part(0, middle), self.part(middle, rows)

    def after(self, *others):
        return Blocks(after(self.array, *[o.array for o in others]), self.stretches)


def after(array, *others):
    return lax.optimization_barrier((array, *others))[0]


def joined(blocks):
    return Blocks(
        jnp.concatenate([b.array for b in blocks], axis=0), [s for b in blocks for s in b.stretches]
    )


def ring(block, axis, size, name, waits={}):
    up, down, got = block, block, []
    for step in range(1, size // 2):
        if step in waits:
            up, down = up.after(*waits[step]), down.after(*waits[step])
        up, down = up.sent(axis, 1, f"{name}_up{step}"), down.sent(axis, -1, f"{name}_down{step}")
        got.append((up, down))
    last = up.halves()[0].sent(axis, 1, f"{name}_up_last"), down.halves()[1].sent(axis, -1, f"{name}_down_last")
    return got, last


def ring_of_pair(one, two, axis, size, name):
    up, down, got = (one, two), (one, two), []
    for step in range(1, size // 2):
        up_one = up[0].sent(axis, 1, f"{name}_up{step}_one")
        down_two = down[1].sent(axis, -1, f"{name}_down{step}_two")
        up_two = up[1].sent(axis, 1, f"{name}_up{step}_two")
        down_one = down[0].sent(axis, -1, f"{name}_down{step}_one")
        up, down = (up_one, up_two), (down_one, down_two)
        got += [up_one, down_two, up_two, down_one]
    return got, [up[0].sent(axis, 1, f"{name}_up_last"), down[1].sent(axis, -1, f"{name}_down_last")]


def project_kernel(stretches, start, place_ref, full_ref, gate_ref, proj_ref, *refs):
    block_refs = refs[: len(stretches)]
    out_ref, grads, weights, gate, total, sem = refs[len(stretches) :]
    shards, k, toks = grads.shape
    rows = weights.shape[1]
    z, x = place_ref[0], place_ref[1]
    per = NZ // PARTS
    copies, parts = [], [[] for _ in range(PARTS)]

    def copy(part, source, target):
        each = pltpu.make_async_copy(source, target, sem.at[len(copies)])
        copies.append(each)
        parts[part].append(each)

    for part in range(PARTS):
        for at in range(part * per, (part + 1) * per):
            copy(part, full_ref.at[lax.rem(z + NZ + DISTANCES[at], NZ), pl.ds(0, k), :], grads.at[at])
        for ref, spans in zip(block_refs, stretches):
            begin = 0
            for dz, dx, row, n in spans:
                at = DISTANCES.index(dz if dz in DISTANCES else dz % NZ)
                if at // per == part:
                    slot = at * NX + lax.rem(x + 2 * NX + dx, NX)
                    copy(part, ref.at[pl.ds(begin, n), :], weights.at[slot, pl.ds(row, n), :])
                begin += n
    copy(PARTS - 1, gate_ref.at[pl.ds(start, rows), :], gate)
    for each in copies:
        each.start()
    out_ref[...] = jnp.zeros_like(out_ref)

    def tile_of(part, at, size):
        tile = pl.ds(at, size)
        hidden = jnp.dot(
            jnp.concatenate([weights[i, tile, :] for i in range(part * per * NX, (part + 1) * per * NX)], axis=1),
            jnp.concatenate([grads[i] for i in range(part * per, (part + 1) * per)], axis=0),
            preferred_element_type=jnp.float32,
        )
        if part:
            hidden += total[tile, :]
        if part < PARTS - 1:
            total[tile, :] = hidden
            return
        up_grad = (hidden * gate[tile, :].astype(jnp.float32)).astype(jnp.bfloat16)
        out_ref[...] += jnp.dot(
            proj_ref[:, pl.ds(start + at, size)], up_grad, preferred_element_type=jnp.float32
        )

    for part in range(PARTS):
        for each in parts[part]:
            each.wait()
        for at in range(0, rows, TILE):
            tile_of(part, at, min(TILE, rows - at))


def project(blocks, full, start, rows, place, gate_t, proj_t):
    toks, rank = gate_t.shape[1], proj_t.shape[0]
    stretches = [b.stretches for b in blocks]
    shards, devices = full.shape[0], NZ * NX
    features = 128 * devices
    n_copies = sum(len(s) for s in stretches) + shards + 1
    any_ref = pl.BlockSpec(memory_space=pl.ANY)
    return pl.pallas_call(
        functools.partial(project_kernel, stretches, start),
        out_shape=jax.ShapeDtypeStruct((rank, toks), jnp.float32),
        in_specs=[pl.BlockSpec(memory_space=pltpu.SMEM), any_ref, any_ref, pl.BlockSpec(memory_space=pltpu.VMEM)]
        + [any_ref] * len(blocks),
        out_specs=pl.BlockSpec(memory_space=pltpu.VMEM),
        scratch_shapes=[
            pltpu.VMEM((shards, features // shards, toks), jnp.bfloat16),
            pltpu.VMEM((devices, rows, 128), jnp.bfloat16),
            pltpu.VMEM((rows, toks), jnp.bfloat16),
            pltpu.VMEM((rows, toks), jnp.float32),
            pltpu.SemaphoreType.DMA((n_copies,)),
        ],
        compiler_params=pltpu.CompilerParams(vmem_limit_bytes=VMEM),
        cost_estimate=pl.CostEstimate(
            flops=2 * toks * rows * (features + 256),
            bytes_accessed=2 * (features * (toks + rows) + toks * rows),
            transcendentals=0,
        ),
    )(place, full, gate_t, proj_t, *[b.array for b in blocks])


def member_of(seq_lengths, tok_rows):
    slots = seq_lengths.shape[0]
    before = lax.iota(jnp.int32, slots)[None, :] < lax.iota(jnp.int32, slots)[:, None]
    starts = jnp.sum(jnp.where(before, seq_lengths[None, :], 0), axis=1)
    ends = starts + seq_lengths
    positions = lax.iota(jnp.int32, tok_rows)
    inside = (positions[None, :] >= starts[:, None]) & (positions[None, :] < ends[:, None])
    return jnp.where(inside, 1.0 / seq_lengths[:, None].astype(jnp.float32), 0.0)


def hand_over(result, assign):
    slots, values = result.shape
    groups = lax.axis_size("dp")
    mine = lax.dynamic_slice_in_dim(assign, lax.axis_index("dp") * slots, slots, 0)
    placing = (mine[None, :] == lax.iota(jnp.int32, slots * groups)[:, None]).astype(jnp.bfloat16)
    spread = jnp.dot(placing, result, preferred_element_type=jnp.float32).astype(jnp.bfloat16)
    got = lax.all_to_all(spread, "dp", split_axis=0, concat_axis=0, tiled=True)
    return jnp.sum(got.reshape(groups, slots, values).astype(jnp.float32), axis=0)


def shards(activations, out_grads, gate_act, w_down, proj_in, proj_out, lengths, assign):
    tok_rows, feat = out_grads.shape
    rank_all = proj_in.shape[1]
    shard_count = lax.axis_size("tensor")
    slots = lengths.shape[1]
    cols = rank_all // shard_count
    group, shard = lax.axis_index("dp"), lax.axis_index("tensor")
    place = jnp.stack([group // NX, group % NX, shard // NC, shard % NC]).astype(jnp.int32)

    in_part = jnp.dot(activations, proj_in, preferred_element_type=jnp.float32)
    in_high = in_part.astype(jnp.bfloat16)
    in_low = (in_part - in_high.astype(jnp.float32)).astype(jnp.bfloat16)
    own = jnp.concatenate([out_grads.T, in_high.T, in_low.T], axis=0)
    own = with_layout_constraint(own, Layout(major_to_minor=(0, 1)))

    rows = w_down.shape[0]
    first = Blocks(w_down[:FIRST], [(0, 0, 0, FIRST)])
    other = Blocks(w_down[FIRST:], [(0, 0, 0, rows - FIRST)])
    first_up, first_down = first.sent("x", 1, "first_x_up"), first.sent("x", -1, "first_x_down")
    first_far = first.sent("x", 2, "first_x_far")
    other_z, other_z_last = ring(other, "z", NZ, "other_z")
    near = joined([other, *other_z[0], other_z[1][0]])
    far = joined([other_z[1][1], *other_z[2], *other_z_last])
    near = near.after(first_up, first_down, first_far)
    far = far.after(first_up, first_down, first_far)
    other_x, other_x_last = ring_of_pair(near, far, "x", NX, "other_x")
    first_x = joined([first, first_up, first_down, first_far]).after(far)
    first_z, first_z_last = ring(first_x, "z", NZ, "first_z", {2: other_x[:2], 3: other_x[2:]})

    full = lax.all_gather(own, "tensor", axis=0)
    full = with_layout_constraint(full, Layout(major_to_minor=(0, 1, 2)))
    in_all = jnp.sum(full[:, feat:].astype(jnp.float32), axis=0)
    in_sum = in_all[:rank_all] + in_all[rank_all:]
    weighted = member_of(lengths[0], tok_rows)[:, None, :] * in_sum[None, :, :]

    proj_t, gate_t = proj_out.T, after(gate_act, other_z_last[0].array).T
    first_all = [first_x, *[b for pair in first_z for b in pair], *first_z_last]
    out_part = project(first_all, full, 0, FIRST, place, gate_t, proj_t)
    other_all = [near, far, *other_x, *other_x_last]
    out_part += project(other_all, full, FIRST, rows - FIRST, place, gate_t, proj_t)

    part = jnp.einsum("cpt,qt->cpq", weighted, out_part, precision=lax.Precision.HIGHEST)
    part = part.reshape(slots, shard_count, cols * rank_all).transpose(1, 0, 2)
    result = jnp.sum(lax.all_to_all(part, "tensor", split_axis=0, concat_axis=0, tiled=True), axis=0)
    return hand_over(result.astype(jnp.bfloat16), assign).reshape(slots, cols, rank_all)


def solution(mesh):
    in_specs = (
        P("dp", "tensor"),
        P("dp", "tensor"),
        P("dp", "tensor"),
        P("tensor", "dp"),
        P("tensor", None),
        P("tensor", None),
        P("dp", None),
        P(),
    )
    out_specs = P("dp", "tensor", None)
    return jax.shard_map(shards, mesh=mesh, in_specs=in_specs, out_specs=out_specs, check_vma=False)
```

time: 291 us -> 183 us (0.63)
  waiting for transfers between devices: 222 us -> 61.9 us
  starting transfers between devices: 4.37 us -> 43.6 us
  Pallas kernels: 0 us -> 25.5 us
  matrix products: 25.2 us -> 4.09 us
  local copies, waits for them, and re-layouts: 3.43 us -> 10.1 us
    all_gather x3 -> x1, waiting for transfers between devices: 214 us -> 0.01 us  [shards(): full = lax.all_gather(own, 'tensor', axis=0)]
    ppermute x0 -> x25, waiting for transfers between devices: none -> 55.8 us  [move(): return lax.ppermute(array, 'dp', pairs)]
    ppermute x0 -> x25, starting transfers between devices: none -> 39.2 us  [move(): return lax.ppermute(array, 'dp', pairs)]
    pallas_call x0 -> x2, Pallas kernels: none -> 25.5 us  [project(): pl.pallas_call(functools.partial(project_kernel, stretches, start), out_s...]
    dot_general x3 -> x2, matrix products: 23.9 us -> 2.78 us  [the longest x1 2.57 us: shards(): jnp.einsum('cpt,qt->cpq', weighted, out_part, precision=lax.Precision.HIG...]
    optimization_barrier x0 -> x1, local copies, waits for them, and re-layouts: none -> 5.61 us  [after(): return lax.optimization_barrier((array, *others))[0]]
  transfers between devices with their start and end apart: 4 -> 27, of which waited for: 4 -> 13; matrix products, arithmetic and copies ran while one was open for 2% -> 5% of each run, Pallas kernels for 0% -> 8%
where the time goes in v2:
time: 183 us
  waiting for transfers between devices  61.9 us (34%)
  starting transfers between devices  43.6 us (24%)
  Pallas kernels  25.5 us (14%)
  blocking collectives  20.1 us (11%)
  between operations  13.7 us (7%)
  local copies, waits for them, and re-layouts  10.1 us (6%)
  matrix products  4.09 us (2%)
  other arithmetic  4.03 us (2%)
    ppermute x25, waiting for transfers between devices, move(): return lax.ppermute(array, 'dp', pairs)  55.8 us
    ppermute x25, starting transfers between devices, move(): return lax.ppermute(array, 'dp', pairs)  39.2 us
    pallas_call x2, Pallas kernels, project(): pl.pallas_call(functools.partial(project_kernel, stretches, start), out_s...  25.5 us
    all_to_all x1, blocking collectives, hand_over(): got = lax.all_to_all(spread, 'dp', split_axis=0, concat_axis=0, tiled=True)  20.1 us
    all_to_all x1, waiting for transfers between devices, shards(): lax.all_to_all(part, 'tensor', split_axis=0, concat_axis=0, tiled=True)  6.05 us
    optimization_barrier x1, local copies, waits for them, and re-layouts, after(): return lax.optimization_barrier((array, *others))[0]  5.61 us
    all_to_all x1, starting transfers between devices, shards(): lax.all_to_all(part, 'tensor', split_axis=0, concat_axis=0, tiled=True)  4.39 us
  transfers between devices with their start and end apart: 27, of which 13 were waited for; matrix products, arithmetic and copies ran while one was open for 5% of the time, Pallas kernels for 8%

profile of v2, /device:TPU:32, one launch (start us, length us, event | category | flops | bytes accessed | tf_op | source)
XLA Modules:
  0.0 183.0 jit_solution(15624538091709577918)
XLA Ops:
  6.5 1.6 copy.14
  8.2 0.0 copy-start.3
  8.2 1.3 subtract_convert_fusion
  9.5 1.2 pad_maximum_fusion
  10.7 0.0 all-gather.3.cloned.1.call-update
  10.7 2.0 %collective-permute-start = (bf16[1024,128]{1,0:T(8,128)(2,1)S(1)}, bf16[1024,128]{1,0:T(8,128)(2,1)S(1)}, u32[]{:S(2)}, u32[]{:S(2)}) collective-permute-start(bf16[1024,128]{1,0:T(8,128)(2,1)S(1)} %slice.30), channel_id=1, source_target_pairs={{0,32},{8,40},{16,48},{24,56},{32,64},{40,72},{48,80},{56,88},{64,... | collective-permute-start | bytes 786440 | tf_op jit(solution)/shard_map/other_z_up1/ppermute | solution.py:22
  12.7 0.1 collective-permute-start.7
  12.8 6.0 %collective-permute-done = bf16[1024,128]{1,0:T(8,128)(2,1)S(1)} collective-permute-done((bf16[1024,128]{1,0:T(8,128)(2,1)S(1)}, bf16[1024,128]{1,0:T(8,128)(2,1)S(1)}, u32[]{:S(2)}, u32[]{:S(2)}) %collective-permute-start) | collective-permute-done | bytes 262176 | tf_op jit(solution)/shard_map/other_z_up1/ppermute | solution.py:22
  18.9 1.9 %collective-permute-start.1 = (bf16[1024,128]{1,0:T(8,128)(2,1)S(1)}, bf16[1024,128]{1,0:T(8,128)(2,1)S(1)}, u32[]{:S(2)}, u32[]{:S(2)}) collective-permute-start(bf16[1024,128]{1,0:T(8,128)(2,1)S(1)} %collective-permute-done), channel_id=1, source_target_pairs={{0,32},{8,40},{16,48},{24,56},{32,64},{40,72},{48,80},{56,88},{64,... | collective-permute-start | bytes 786440 | tf_op jit(solution)/shard_map/other_z_up2/ppermute | solution.py:22
  20.8 2.3 %collective-permute-start.8 = (bf16[1024,128]{1,0:T(8,128)(2,1)S(1)}, bf16[1024,128]{1,0:T(8,128)(2,1)S(1)}, u32[]{:S(2)}, u32[]{:S(2)}) collective-permute-start(bf16[1024,128]{1,0:T(8,128)(2,1)S(1)} %collective-permute-done.7), channel_id=1, source_target_pairs={{0,224},{8,232},{16,240},{24,248},{32,0},{40,8},{48,16},{56,24},{6... | collective-permute-start | bytes 786440 | tf_op jit(solution)/shard_map/other_z_down2/ppermute | solution.py:22
  23.1 1.6 collective-permute-start.4
  24.7 1.7 collective-permute-start.5
  26.4 1.8 collective-permute-start.6
  28.2 0.6 collective-permute-done.1
  28.8 0.1 collective-permute-start.2
  29.0 0.3 collective-permute-done.8
  29.2 2.6 %collective-permute-start.9 = (bf16[1024,128]{1,0:T(8,128)(2,1)S(1)}, bf16[1024,128]{1,0:T(8,128)(2,1)S(1)}, u32[]{:S(2)}, u32[]{:S(2)}) collective-permute-start(bf16[1024,128]{1,0:T(8,128)(2,1)S(1)} %collective-permute-done.8), channel_id=1, source_target_pairs={{0,224},{8,232},{16,240},{24,248},{32,0},{40,8},{48,16},{56,24},{6... | collective-permute-start | bytes 786440 | tf_op jit(solution)/shard_map/other_z_down3/ppermute | solution.py:22
  31.8 0.1 pad_maximum_fusion.1.refs_0_
  31.9 0.0 copy-start.11
  31.9 0.0 collective-permute-done.4
  31.9 1.8 collective-permute-done.5
  33.7 1.7 collective-permute-done.6
  35.4 1.1 collective-permute-start.13
  36.6 0.0 collective-permute-done.2
  36.6 0.7 collective-permute-start.3
  37.4 2.4 %collective-permute-start.10 = (bf16[512,128]{1,0:T(8,128)(2,1)S(1)}, bf16[512,128]{1,0:T(8,128)(2,1)S(1)}, u32[]{:S(2)}, u32[]{:S(2)}) collective-permute-start(bf16[512,128]{1,0:T(8,128)(2,1)S(1)} %slice.40), channel_id=1, source_target_pairs={{0,224},{8,232},{16,240},{24,248},{32,0},{40,8},{48,16},{56,24},{6... | collective-permute-start | bytes 393224 | tf_op jit(solution)/shard_map/other_z_down_last/ppermute | solution.py:22
  39.9 2.7 %collective-permute-done.3 = bf16[512,128]{1,0:T(8,128)(2,1)S(1)} collective-permute-done((bf16[512,128]{1,0:T(8,128)(2,1)S(1)}, bf16[512,128]{1,0:T(8,128)(2,1)S(1)}, u32[]{:S(2)}, u32[]{:S(2)}) %collective-permute-start.3) | collective-permute-done | bytes 131104 | tf_op jit(solution)/shard_map/other_z_up_last/ppermute | solution.py:22
  42.6 0.7 collective-permute-done.10
  43.4 2.3 %collective-permute-start.14 = (bf16[4096,128]{1,0:T(8,128)(2,1)S(1)}, bf16[4096,128]{1,0:T(8,128)(2,1)}, u32[]{:S(2)}, u32[]{:S(2)}) collective-permute-start(bf16[4096,128]{1,0:T(8,128)(2,1)S(1)} %constant_dynamic-update-slice_fusion.refs_1_), channel_id=1, source_target_pairs={{0,24},{8,0},{16,8},{24,16},{32,56},{40,32},{48,40},{56,48},{64,88... | collective-permute-start | bytes 3145736 | tf_op jit(solution)/shard_map/other_x_down1_two/ppermute | solution.py:25
  45.7 0.1 pad_maximum_fusion.2.refs_0_
  45.8 3.1 %collective-permute-start.12 = (bf16[3072,128]{1,0:T(8,128)(2,1)S(1)}, bf16[3072,128]{1,0:T(8,128)(2,1)S(1)}, u32[]{:S(2)}, u32[]{:S(2)}) collective-permute-start(bf16[3072,128]{1,0:T(8,128)(2,1)S(1)} %pad_maximum_fusion.2.refs_0_), channel_id=1, source_target_pairs={{0,224},{8,232},{16,240},{24,248},{32,0},{40,8},{48,16},{56,24},{6... | collective-permute-start | bytes 2359304 | tf_op jit(solution)/shard_map/first_z_down1/ppermute | solution.py:22
  48.9 0.5 collective-permute-start.11
  49.4 0.8 collective-permute-start.18
  50.3 9.6 %collective-permute-done.13.refs_2_ = bf16[4096,128]{1,0:T(8,128)(2,1)} collective-permute-done((bf16[4096,128]{1,0:T(8,128)(2,1)S(1)}, bf16[4096,128]{1,0:T(8,128)(2,1)}, u32[]{:S(2)}, u32[]{:S(2)}) %collective-permute-start.13) | collective-permute-done | bytes 1048608 | tf_op jit(solution)/shard_map/other_x_up1_one/ppermute | solution.py:25
  59.9 3.2 %collective-permute-done.12.refs_2_ = bf16[3072,128]{1,0:T(8,128)(2,1)S(1)} collective-permute-done((bf16[3072,128]{1,0:T(8,128)(2,1)S(1)}, bf16[3072,128]{1,0:T(8,128)(2,1)S(1)}, u32[]{:S(2)}, u32[]{:S(2)}) %collective-permute-start.12) | collective-permute-done | bytes 786464 | tf_op jit(solution)/shard_map/first_z_down1/ppermute | solution.py:22
  63.1 6.5 %collective-permute-done.14.refs_3_ = bf16[4096,128]{1,0:T(8,128)(2,1)} collective-permute-done((bf16[4096,128]{1,0:T(8,128)(2,1)S(1)}, bf16[4096,128]{1,0:T(8,128)(2,1)}, u32[]{:S(2)}, u32[]{:S(2)}) %collective-permute-start.14) | collective-permute-done | bytes 1048608 | tf_op jit(solution)/shard_map/other_x_down1_two/ppermute | solution.py:25
  69.7 2.7 %collective-permute-start.16 = (bf16[3072,128]{1,0:T(8,128)(2,1)S(1)}, bf16[3072,128]{1,0:T(8,128)(2,1)}, u32[]{:S(2)}, u32[]{:S(2)}) collective-permute-start(bf16[3072,128]{1,0:T(8,128)(2,1)S(1)} %collective-permute-done.12.refs_2_), channel_id=1, source_target_pairs={{0,224},{8,232},{16,240},{24,248},{32,0},{40,8},{48,16},{56,24},{6... | collective-permute-start | bytes 2359304 | tf_op jit(solution)/shard_map/first_z_down2/ppermute | solution.py:22
  72.4 0.3 collective-permute-start.15
  72.6 1.3 collective-permute-start.23
  73.9 13.7 %collective-permute-done.18.refs_5_ = bf16[4096,128]{1,0:T(8,128)(2,1)S(1)} collective-permute-done((bf16[4096,128]{1,0:T(8,128)(2,1)S(1)}, bf16[4096,128]{1,0:T(8,128)(2,1)S(1)}, u32[]{:S(2)}, u32[]{:S(2)}) %collective-permute-start.18) | collective-permute-done | bytes 1048608 | tf_op jit(solution)/shard_map/other_x_down1_one/ppermute | solution.py:25
  87.7 1.0 copy-done.8
  88.6 3.7 %collective-permute-start.24 = (bf16[4096,128]{1,0:T(8,128)(2,1)}, bf16[4096,128]{1,0:T(8,128)(2,1)}, u32[]{:S(2)}, u32[]{:S(2)}) collective-permute-start(bf16[4096,128]{1,0:T(8,128)(2,1)} %collective-permute-done.14.refs_3_), channel_id=1, source_target_pairs={{0,24},{8,0},{16,8},{24,16},{32,56},{40,32},{48,40},{56,48},{64,88... | collective-permute-start | bytes 3145736 | tf_op jit(solution)/shard_map/other_x_down_last/ppermute | solution.py:25
  92.4 3.0 %collective-permute-start.20 = (bf16[3072,128]{1,0:T(8,128)(2,1)}, bf16[3072,128]{1,0:T(8,128)(2,1)S(1)}, u32[]{:S(2)}, u32[]{:S(2)}) collective-permute-start(bf16[3072,128]{1,0:T(8,128)(2,1)} %collective-permute-done.16.refs_4_), channel_id=1, source_target_pairs={{0,224},{8,232},{16,240},{24,248},{32,0},{40,8},{48,16},{56,24},{6... | collective-permute-start | bytes 2359304 | tf_op jit(solution)/shard_map/first_z_down3/ppermute | solution.py:22
  95.4 0.1 collective-permute-start.19
  95.5 0.7 pad_add_fusion.place_ref
  96.2 0.1 select_reduce_fusion
  96.3 0.1 fusion.9
  96.4 5.6 %copy.15 = bf16[896,1792]{0,1:T(8,128)(2,1)} copy(bf16[896,1792]{1,0:T(8,128)(2,1)} %param.10) | data formatting | bytes 6422528 | tf_op jit(solution)/shard_map/optimization_barrier | solution.py:62
  102.0 8.7 %collective-permute-done.20.refs_6_ = bf16[3072,128]{1,0:T(8,128)(2,1)S(1)} collective-permute-done((bf16[3072,128]{1,0:T(8,128)(2,1)}, bf16[3072,128]{1,0:T(8,128)(2,1)S(1)}, u32[]{:S(2)}, u32[]{:S(2)}) %collective-permute-start.20) | collective-permute-done | bytes 786464 | tf_op jit(solution)/shard_map/first_z_down3/ppermute | solution.py:22
  110.7 2.5 %collective-permute-start.22 = (bf16[1536,128]{1,0:T(8,128)(2,1)S(1)}, bf16[1536,128]{1,0:T(8,128)(2,1)}, u32[]{:S(2)}, u32[]{:S(2)}) collective-permute-start(bf16[1536,128]{1,0:T(8,128)(2,1)S(1)} %slice.42), channel_id=1, source_target_pairs={{0,224},{8,232},{16,240},{24,248},{32,0},{40,8},{48,16},{56,24},{6... | collective-permute-start | bytes 1179656 | tf_op jit(solution)/shard_map/first_z_down_last/ppermute | solution.py:22
  113.2 0.4 collective-permute-start.21
  113.7 14.1 %shard_map.83 = f32[64,896]{1,0:T(8,128)} custom-call(s32[4]{0:T(128)} %pad_add_fusion.place_ref, bf16[8,640,896]{2,1,0:T(8,128)(2,1)} %bitcast.25, bf16[1792,896]{1,0:T(8,128)(2,1)} %bitcast.23, bf16[64,1792]{1,0:T(8,128)(2,1)} %bitcast.28, bf16[4096,128]{1,0:T(8,128)(2,1)} %copy-done.1, bf16[4096,128]{1,0:T(8,128)(2,1)} %copy-done.7, ...), custom_call_target="tpu_custom_call" | custom-call | flops 7985954816 | bytes 17563648 | tf_op jit(solution)/shard_map/pallas_call | solution.py:155
  127.8 1.8 convert_reduce_fusion
  129.7 0.0 copy-start.10
  129.7 11.4 %shard_map.82 = f32[64,896]{1,0:T(8,128)} custom-call(s32[4]{0:T(128)} %pad_add_fusion.place_ref, bf16[8,640,896]{2,1,0:T(8,128)(2,1)} %bitcast.27, bf16[1792,896]{1,0:T(8,128)(2,1)} %bitcast.24, bf16[64,1792]{1,0:T(8,128)(2,1)} %bitcast.29, bf16[3072,128]{1,0:T(8,128)(2,1)} %copy-done.2, bf16[3072,128]{1,0:T(8,128)(2,1)} %collective-permute-done.11.refs_1_, ...), custom_call_target="tpu_custom_call" | custom-call | flops 5989466112 | bytes 15007744 | tf_op jit(solution)/shard_map/pallas_call | solution.py:155
  141.1 2.6 %fusion = f32[8,64,64]{2,1,0:T(8,128)S(1)} fusion(f32[64,896]{1,0:T(8,128)S(1)} %slice_add_fusion, f32[8,896]{1,0:T(8,128)S(1)} %fusion.9, f32[64,896]{1,0:T(8,128)} %shard_map.82, f32[64,896]{1,0:T(8,128)S(1)} %copy-done.4), kind=kOutput, calls=%fused_computation.1 | convolution fusion | flops 352837632 | bytes 847872 | tf_op jit(solution)/shard_map/cpt,qt->cpq/dot_general | solution.py:238
  143.7 0.1 reshape.75
  143.8 0.7 copy.18
  144.5 4.4 %all-to-all-start = ((f32[8,8,512]{2,1,0:T(8,128)}), f32[8,8,512]{2,1,0:T(8,128)S(1)}, u32[]{:S(2)}, u32[]{:S(2)}) async-start(f32[8,8,512]{2,1,0:T(8,128)} %bitcast.21), calls=%async_computation | async-start | bytes 262144 | tf_op jit(solution)/shard_map/all_to_all | solution.py:240
  148.9 0.1 dynamic_slice.3
  149.0 6.1 %all-to-all-done = f32[8,8,512]{2,1,0:T(8,128)S(1)} async-done(((f32[8,8,512]{2,1,0:T(8,128)}), f32[8,8,512]{2,1,0:T(8,128)S(1)}, u32[]{:S(2)}, u32[]{:S(2)}) %all-to-all-start) | async-done | bytes 131104 | tf_op jit(solution)/shard_map/all_to_all | solution.py:240
  155.1 0.2 fusion.2
  155.3 20.1 %all_to_all.14 = bf16[32,8,512]{2,1,0:T(8,128)(2,1)S(1)} all-to-all(bf16[32,8,512]{2,1,0:T(8,128)(2,1)S(1)} %fusion.2), channel_id=1, replica_groups=mesh['dp'=32,'tensor'=8] {'dp'}, dimensions={0} | all-to-all | bytes 524288 | tf_op jit(solution)/shard_map/all_to_all | solution.py:193
  175.4 0.7 reshape.76
  (50 shorter events, 0.4 us)
Async XLA Ops:
  6.5 1.6 copy-start
  6.5 107.1 %all-gather.3.cloned.1.call-start = ((), (), s32[]{:S(2)}) async-start(), calls=%async_computation.2 | async-start | bytes 10321920 | tf_op jit(solution)/shard_map/all_gather | solution.py:226
  8.2 2.5 %copy-start.3 = (bf16[1792,128]{1,0:T(8,128)(2,1)S(1)}, bf16[1792,128]{1,0:T(8,128)(2,1)}, u32[]{:S(2)}) copy-start(bf16[1792,128]{1,0:T(8,128)(2,1)} %param.11) | copy-start | bytes 1376260
  10.7 8.1 %collective-permute-start = (bf16[1024,128]{1,0:T(8,128)(2,1)S(1)}, bf16[1024,128]{1,0:T(8,128)(2,1)S(1)}, u32[]{:S(2)}, u32[]{:S(2)}) collective-permute-start(bf16[1024,128]{1,0:T(8,128)(2,1)S(1)} %slice.30), channel_id=1, source_target_pairs={{0,32},{8,40},{16,48},{24,56},{32,64},{40,72},{48,80},{56,88},{64,... | collective-permute-start | bytes 786440 | tf_op jit(solution)/shard_map/other_z_up1/ppermute | solution.py:22
  12.7 8.0 %collective-permute-start.7 = (bf16[1024,128]{1,0:T(8,128)(2,1)S(1)}, bf16[1024,128]{1,0:T(8,128)(2,1)S(1)}, u32[]{:S(2)}, u32[]{:S(2)}) collective-permute-start(bf16[1024,128]{1,0:T(8,128)(2,1)S(1)} %slice.30), channel_id=1, source_target_pairs={{0,224},{8,232},{16,240},{24,248},{32,0},{40,8},{48,16},{56,24},{6... | collective-permute-start | bytes 786440 | tf_op jit(solution)/shard_map/other_z_down1/ppermute | solution.py:22
  18.9 10.0 %collective-permute-start.1 = (bf16[1024,128]{1,0:T(8,128)(2,1)S(1)}, bf16[1024,128]{1,0:T(8,128)(2,1)S(1)}, u32[]{:S(2)}, u32[]{:S(2)}) collective-permute-start(bf16[1024,128]{1,0:T(8,128)(2,1)S(1)} %collective-permute-done), channel_id=1, source_target_pairs={{0,32},{8,40},{16,48},{24,56},{32,64},{40,72},{48,80},{56,88},{64,... | collective-permute-start | bytes 786440 | tf_op jit(solution)/shard_map/other_z_up2/ppermute | solution.py:22
  20.8 8.5 %collective-permute-start.8 = (bf16[1024,128]{1,0:T(8,128)(2,1)S(1)}, bf16[1024,128]{1,0:T(8,128)(2,1)S(1)}, u32[]{:S(2)}, u32[]{:S(2)}) collective-permute-start(bf16[1024,128]{1,0:T(8,128)(2,1)S(1)} %collective-permute-done.7), channel_id=1, source_target_pairs={{0,224},{8,232},{16,240},{24,248},{32,0},{40,8},{48,16},{56,24},{6... | collective-permute-start | bytes 786440 | tf_op jit(solution)/shard_map/other_z_down2/ppermute | solution.py:22
  23.1 8.8 %collective-permute-start.4 = (bf16[768,128]{1,0:T(8,128)(2,1)S(1)}, bf16[768,128]{1,0:T(8,128)(2,1)S(1)}, u32[]{:S(2)}, u32[]{:S(2)}) collective-permute-start(bf16[768,128]{1,0:T(8,128)(2,1)S(1)} %slice.32), channel_id=1, source_target_pairs={{0,8},{8,16},{16,24},{24,0},{32,40},{40,48},{48,56},{56,32},{64,72... | collective-permute-start | bytes 589832 | tf_op jit(solution)/shard_map/first_x_up/ppermute | solution.py:25
  24.7 9.0 %collective-permute-start.5 = (bf16[768,128]{1,0:T(8,128)(2,1)S(1)}, bf16[768,128]{1,0:T(8,128)(2,1)S(1)}, u32[]{:S(2)}, u32[]{:S(2)}) collective-permute-start(bf16[768,128]{1,0:T(8,128)(2,1)S(1)} %slice.32), channel_id=1, source_target_pairs={{0,24},{8,0},{16,8},{24,16},{32,56},{40,32},{48,40},{56,48},{64,88... | collective-permute-start | bytes 589832 | tf_op jit(solution)/shard_map/first_x_down/ppermute | solution.py:25
  26.4 9.0 %collective-permute-start.6 = (bf16[768,128]{1,0:T(8,128)(2,1)S(1)}, bf16[768,128]{1,0:T(8,128)(2,1)S(1)}, u32[]{:S(2)}, u32[]{:S(2)}) collective-permute-start(bf16[768,128]{1,0:T(8,128)(2,1)S(1)} %slice.32), channel_id=1, source_target_pairs={{0,16},{8,24},{16,0},{24,8},{32,48},{40,56},{48,32},{56,40},{64,80... | collective-permute-start | bytes 589832 | tf_op jit(solution)/shard_map/first_x_far/ppermute | solution.py:25
  28.8 7.8 %collective-permute-start.2 = (bf16[1024,128]{1,0:T(8,128)(2,1)S(1)}, bf16[1024,128]{1,0:T(8,128)(2,1)S(1)}, u32[]{:S(2)}, u32[]{:S(2)}) collective-permute-start(bf16[1024,128]{1,0:T(8,128)(2,1)S(1)} %collective-permute-done.1), channel_id=1, source_target_pairs={{0,32},{8,40},{16,48},{24,56},{32,64},{40,72},{48,80},{56,88},{64,... | collective-permute-start | bytes 786440 | tf_op jit(solution)/shard_map/other_z_up3/ppermute | solution.py:22
  29.2 8.1 %collective-permute-start.9 = (bf16[1024,128]{1,0:T(8,128)(2,1)S(1)}, bf16[1024,128]{1,0:T(8,128)(2,1)S(1)}, u32[]{:S(2)}, u32[]{:S(2)}) collective-permute-start(bf16[1024,128]{1,0:T(8,128)(2,1)S(1)} %collective-permute-done.8), channel_id=1, source_target_pairs={{0,224},{8,232},{16,240},{24,248},{32,0},{40,8},{48,16},{56,24},{6... | collective-permute-start | bytes 786440 | tf_op jit(solution)/shard_map/other_z_down3/ppermute | solution.py:22
  31.9 17.6 %copy-start.1 = (bf16[4096,128]{1,0:T(8,128)(2,1)}, bf16[4096,128]{1,0:T(8,128)(2,1)S(1)}, u32[]{:S(2)}) copy-start(bf16[4096,128]{1,0:T(8,128)(2,1)S(1)} %pad_maximum_fusion.1.refs_0_) | copy-start | bytes 3145732
  31.9 64.3 %copy-start.11 = (s32[1,8]{1,0:T(1,128)S(1)}, s32[1,8]{1,0:T(1,128)}, u32[]{:S(2)}) copy-start(s32[1,8]{1,0:T(1,128)} %param.14) | copy-start | bytes 100
  35.4 24.5 %collective-permute-start.13 = (bf16[4096,128]{1,0:T(8,128)(2,1)S(1)}, bf16[4096,128]{1,0:T(8,128)(2,1)}, u32[]{:S(2)}, u32[]{:S(2)}) collective-permute-start(bf16[4096,128]{1,0:T(8,128)(2,1)S(1)} %pad_maximum_fusion.1.refs_0_), channel_id=1, source_target_pairs={{0,8},{8,16},{16,24},{24,0},{32,40},{40,48},{48,56},{56,32},{64,72... | collective-permute-start | bytes 3145736 | tf_op jit(solution)/shard_map/other_x_up1_one/ppermute | solution.py:25
  36.6 6.0 %collective-permute-start.3 = (bf16[512,128]{1,0:T(8,128)(2,1)S(1)}, bf16[512,128]{1,0:T(8,128)(2,1)S(1)}, u32[]{:S(2)}, u32[]{:S(2)}) collective-permute-start(bf16[512,128]{1,0:T(8,128)(2,1)S(1)} %slice.39), channel_id=1, source_target_pairs={{0,32},{8,40},{16,48},{24,56},{32,64},{40,72},{48,80},{56,88},{64,... | collective-permute-start | bytes 393224 | tf_op jit(solution)/shard_map/other_z_up_last/ppermute | solution.py:22
  37.4 6.0 %collective-permute-start.10 = (bf16[512,128]{1,0:T(8,128)(2,1)S(1)}, bf16[512,128]{1,0:T(8,128)(2,1)S(1)}, u32[]{:S(2)}, u32[]{:S(2)}) collective-permute-start(bf16[512,128]{1,0:T(8,128)(2,1)S(1)} %slice.40), channel_id=1, source_target_pairs={{0,224},{8,232},{16,240},{24,248},{32,0},{40,8},{48,16},{56,24},{6... | collective-permute-start | bytes 393224 | tf_op jit(solution)/shard_map/other_z_down_last/ppermute | solution.py:22
  43.4 49.0 %copy-start.7 = (bf16[4096,128]{1,0:T(8,128)(2,1)}, bf16[4096,128]{1,0:T(8,128)(2,1)S(1)}, u32[]{:S(2)}) copy-start(bf16[4096,128]{1,0:T(8,128)(2,1)S(1)} %constant_dynamic-update-slice_fusion.refs_1_) | copy-start | bytes 3145732
  43.4 26.3 %collective-permute-start.14 = (bf16[4096,128]{1,0:T(8,128)(2,1)S(1)}, bf16[4096,128]{1,0:T(8,128)(2,1)}, u32[]{:S(2)}, u32[]{:S(2)}) collective-permute-start(bf16[4096,128]{1,0:T(8,128)(2,1)S(1)} %constant_dynamic-update-slice_fusion.refs_1_), channel_id=1, source_target_pairs={{0,24},{8,0},{16,8},{24,16},{32,56},{40,32},{48,40},{56,48},{64,88... | collective-permute-start | bytes 3145736 | tf_op jit(solution)/shard_map/other_x_down1_two/ppermute | solution.py:25
  45.7 56.2 %copy-start.2 = (bf16[3072,128]{1,0:T(8,128)(2,1)}, bf16[3072,128]{1,0:T(8,128)(2,1)S(1)}, u32[]{:S(2)}) copy-start(bf16[3072,128]{1,0:T(8,128)(2,1)S(1)} %pad_maximum_fusion.2.refs_0_) | copy-start | bytes 2359300
  45.8 17.4 %collective-permute-start.12 = (bf16[3072,128]{1,0:T(8,128)(2,1)S(1)}, bf16[3072,128]{1,0:T(8,128)(2,1)S(1)}, u32[]{:S(2)}, u32[]{:S(2)}) collective-permute-start(bf16[3072,128]{1,0:T(8,128)(2,1)S(1)} %pad_maximum_fusion.2.refs_0_), channel_id=1, source_target_pairs={{0,224},{8,232},{16,240},{24,248},{32,0},{40,8},{48,16},{56,24},{6... | collective-permute-start | bytes 2359304 | tf_op jit(solution)/shard_map/first_z_down1/ppermute | solution.py:22
  48.9 23.5 %collective-permute-start.11 = (bf16[3072,128]{1,0:T(8,128)(2,1)S(1)}, bf16[3072,128]{1,0:T(8,128)(2,1)}, u32[]{:S(2)}, u32[]{:S(2)}) collective-permute-start(bf16[3072,128]{1,0:T(8,128)(2,1)S(1)} %pad_maximum_fusion.2.refs_0_), channel_id=1, source_target_pairs={{0,32},{8,40},{16,48},{24,56},{32,64},{40,72},{48,80},{56,88},{64,... | collective-permute-start | bytes 2359304 | tf_op jit(solution)/shard_map/first_z_up1/ppermute | solution.py:22
  49.4 38.2 %collective-permute-start.18 = (bf16[4096,128]{1,0:T(8,128)(2,1)S(1)}, bf16[4096,128]{1,0:T(8,128)(2,1)S(1)}, u32[]{:S(2)}, u32[]{:S(2)}) collective-permute-start(bf16[4096,128]{1,0:T(8,128)(2,1)S(1)} %pad_maximum_fusion.1.refs_0_), channel_id=1, source_target_pairs={{0,24},{8,0},{16,8},{24,16},{32,56},{40,32},{48,40},{56,48},{64,88... | collective-permute-start | bytes 3145736 | tf_op jit(solution)/shard_map/other_x_down1_one/ppermute | solution.py:25
  59.9 32.5 %collective-permute-start.17 = (bf16[4096,128]{1,0:T(8,128)(2,1)S(1)}, bf16[4096,128]{1,0:T(8,128)(2,1)}, u32[]{:S(2)}, u32[]{:S(2)}) collective-permute-start(bf16[4096,128]{1,0:T(8,128)(2,1)S(1)} %constant_dynamic-update-slice_fusion.refs_1_), channel_id=1, source_target_pairs={{0,8},{8,16},{16,24},{24,0},{32,40},{40,48},{48,56},{56,32},{64,72... | collective-permute-start | bytes 3145736 | tf_op jit(solution)/shard_map/other_x_up1_two/ppermute | solution.py:25
  63.1 32.3 %copy-start.9 = (bf16[3072,128]{1,0:T(8,128)(2,1)}, bf16[3072,128]{1,0:T(8,128)(2,1)S(1)}, u32[]{:S(2)}) copy-start(bf16[3072,128]{1,0:T(8,128)(2,1)S(1)} %collective-permute-done.12.refs_2_) | copy-start | bytes 2359300
  69.7 22.7 %collective-permute-start.16 = (bf16[3072,128]{1,0:T(8,128)(2,1)S(1)}, bf16[3072,128]{1,0:T(8,128)(2,1)}, u32[]{:S(2)}, u32[]{:S(2)}) collective-permute-start(bf16[3072,128]{1,0:T(8,128)(2,1)S(1)} %collective-permute-done.12.refs_2_), channel_id=1, source_target_pairs={{0,224},{8,232},{16,240},{24,248},{32,0},{40,8},{48,16},{56,24},{6... | collective-permute-start | bytes 2359304 | tf_op jit(solution)/shard_map/first_z_down2/ppermute | solution.py:22
  72.4 23.0 %collective-permute-start.15 = (bf16[3072,128]{1,0:T(8,128)(2,1)}, bf16[3072,128]{1,0:T(8,128)(2,1)}, u32[]{:S(2)}, u32[]{:S(2)}) collective-permute-start(bf16[3072,128]{1,0:T(8,128)(2,1)} %collective-permute-done.11.refs_1_), channel_id=1, source_target_pairs={{0,32},{8,40},{16,48},{24,56},{32,64},{40,72},{48,80},{56,88},{64,... | collective-permute-start | bytes 2359304 | tf_op jit(solution)/shard_map/first_z_up2/ppermute | solution.py:22
  72.6 41.0 %collective-permute-start.23 = (bf16[4096,128]{1,0:T(8,128)(2,1)}, bf16[4096,128]{1,0:T(8,128)(2,1)}, u32[]{:S(2)}, u32[]{:S(2)}) collective-permute-start(bf16[4096,128]{1,0:T(8,128)(2,1)} %collective-permute-done.13.refs_2_), channel_id=1, source_target_pairs={{0,8},{8,16},{16,24},{24,0},{32,40},{40,48},{48,56},{56,32},{64,72... | collective-permute-start | bytes 3145736 | tf_op jit(solution)/shard_map/other_x_up_last/ppermute | solution.py:25
  87.7 1.0 copy-start.8
  88.6 25.0 %collective-permute-start.24 = (bf16[4096,128]{1,0:T(8,128)(2,1)}, bf16[4096,128]{1,0:T(8,128)(2,1)}, u32[]{:S(2)}, u32[]{:S(2)}) collective-permute-start(bf16[4096,128]{1,0:T(8,128)(2,1)} %collective-permute-done.14.refs_3_), channel_id=1, source_target_pairs={{0,24},{8,0},{16,8},{24,16},{32,56},{40,32},{48,40},{56,48},{64,88... | collective-permute-start | bytes 3145736 | tf_op jit(solution)/shard_map/other_x_down_last/ppermute | solution.py:25
  92.4 18.4 %collective-permute-start.20 = (bf16[3072,128]{1,0:T(8,128)(2,1)}, bf16[3072,128]{1,0:T(8,128)(2,1)S(1)}, u32[]{:S(2)}, u32[]{:S(2)}) collective-permute-start(bf16[3072,128]{1,0:T(8,128)(2,1)} %collective-permute-done.16.refs_4_), channel_id=1, source_target_pairs={{0,224},{8,232},{16,240},{24,248},{32,0},{40,8},{48,16},{56,24},{6... | collective-permute-start | bytes 2359304 | tf_op jit(solution)/shard_map/first_z_down3/ppermute | solution.py:22
  95.4 17.8 %collective-permute-start.19 = (bf16[3072,128]{1,0:T(8,128)(2,1)}, bf16[3072,128]{1,0:T(8,128)(2,1)S(1)}, u32[]{:S(2)}, u32[]{:S(2)}) collective-permute-start(bf16[3072,128]{1,0:T(8,128)(2,1)} %collective-permute-done.15.refs_3_), channel_id=1, source_target_pairs={{0,32},{8,40},{16,48},{24,56},{32,64},{40,72},{48,80},{56,88},{64,... | collective-permute-start | bytes 2359304 | tf_op jit(solution)/shard_map/first_z_up3/ppermute | solution.py:22
  110.7 17.1 %copy-start.5 = (bf16[3072,128]{1,0:T(8,128)(2,1)}, bf16[3072,128]{1,0:T(8,128)(2,1)S(1)}, u32[]{:S(2)}) copy-start(bf16[3072,128]{1,0:T(8,128)(2,1)S(1)} %collective-permute-done.20.refs_6_) | copy-start | bytes 2359300
  110.7 19.0 %collective-permute-start.22 = (bf16[1536,128]{1,0:T(8,128)(2,1)S(1)}, bf16[1536,128]{1,0:T(8,128)(2,1)}, u32[]{:S(2)}, u32[]{:S(2)}) collective-permute-start(bf16[1536,128]{1,0:T(8,128)(2,1)S(1)} %slice.42), channel_id=1, source_target_pairs={{0,224},{8,232},{16,240},{24,248},{32,0},{40,8},{48,16},{56,24},{6... | collective-permute-start | bytes 1179656 | tf_op jit(solution)/shard_map/first_z_down_last/ppermute | solution.py:22
  113.2 14.6 %copy-start.6 = (bf16[3072,128]{1,0:T(8,128)(2,1)}, bf16[3072,128]{1,0:T(8,128)(2,1)S(1)}, u32[]{:S(2)}) copy-start(bf16[3072,128]{1,0:T(8,128)(2,1)S(1)} %collective-permute-done.19.refs_5_) | copy-start | bytes 2359300
  113.2 16.5 %collective-permute-start.21 = (bf16[1536,128]{1,0:T(8,128)(2,1)S(1)}, bf16[1536,128]{1,0:T(8,128)(2,1)}, u32[]{:S(2)}, u32[]{:S(2)}) collective-permute-start(bf16[1536,128]{1,0:T(8,128)(2,1)S(1)} %slice.41), channel_id=1, source_target_pairs={{0,32},{8,40},{16,48},{24,56},{32,64},{40,72},{48,80},{56,88},{64,... | collective-permute-start | bytes 1179656 | tf_op jit(solution)/shard_map/first_z_up_last/ppermute | solution.py:22
  129.7 11.4 %copy-start.4 = (f32[64,896]{1,0:T(8,128)S(1)}, f32[64,896]{1,0:T(8,128)}, u32[]{:S(2)}) copy-start(f32[64,896]{1,0:T(8,128)} %shard_map.83) | copy-start | bytes 688132
  129.7 19.2 %copy-start.10 = (s32[256]{0:T(256)S(1)}, s32[256]{0:T(256)}, u32[]{:S(2)}) copy-start(s32[256]{0:T(256)} %param.15) | copy-start | bytes 3076
  144.5 10.5 %all-to-all-start = ((f32[8,8,512]{2,1,0:T(8,128)}), f32[8,8,512]{2,1,0:T(8,128)S(1)}, u32[]{:S(2)}, u32[]{:S(2)}) async-start(f32[8,8,512]{2,1,0:T(8,128)} %bitcast.21), calls=%async_computation | async-start | bytes 262144 | tf_op jit(solution)/shard_map/all_to_all | solution.py:240
Sparse Core Ops, SparseCore 0:
  10.8 58.1 all-gather.2

commit v3 on v2

--- a/solution.py
+++ b/solution.py
@@ -9,11 +9,11 @@
 from jax.sharding import PartitionSpec as P
 
 NZ, NX, NY, NC = 8, 4, 4, 2
-TILE = 384
+TILE = 512
 DISTANCES = (0, -1, 1, -2, 2, -3, 3, 4)
 PARTS = 4
 VMEM = 58 * 2**20
-FIRST = 768
+FIRST = 896
 
 
 def move(array, axis, dist):

time: 183 us -> 182 us (level)
  waiting for transfers between devices: 61.9 us -> 60 us
    ppermute x25, waiting for transfers between devices: 55.8 us -> 53.9 us  [move(): return lax.ppermute(array, 'dp', pairs)]
  transfers between devices with their start and end apart: 27 -> 27, of which waited for: 13 -> 15; matrix products, arithmetic and copies ran while one was open for 5% -> 5% of each run, Pallas kernels for 8% -> 7%
where the time goes in v3:
time: 182 us; the launch traced here: 181 us
  waiting for transfers between devices  60 us (33%)
  starting transfers between devices  43 us (24%)
  Pallas kernels  25.1 us (14%)
  blocking collectives  21.4 us (12%)
  between operations  13.7 us (8%)
  local copies, waits for them, and re-layouts  11 us (6%)
  other arithmetic  3.88 us (2%)
  matrix products  3.21 us (2%)
    ppermute x25, waiting for transfers between devices, move(): return lax.ppermute(array, 'dp', pairs)  53.9 us
    ppermute x25, starting transfers between devices, move(): return lax.ppermute(array, 'dp', pairs)  38.7 us
    pallas_call x2, Pallas kernels, project(): pl.pallas_call(functools.partial(project_kernel, stretches, start), out_s...  25.1 us
    all_to_all x1, blocking collectives, hand_over(): got = lax.all_to_all(spread, 'dp', split_axis=0, concat_axis=0, tiled=True)  21.4 us
    all_to_all x1, waiting for transfers between devices, shards(): lax.all_to_all(part, 'tensor', split_axis=0, concat_axis=0, tiled=True)  6.05 us
    optimization_barrier x1, local copies, waits for them, and re-layouts, after(): return lax.optimization_barrier((array, *others))[0]  5.62 us
    all_to_all x1, starting transfers between devices, shards(): lax.all_to_all(part, 'tensor', split_axis=0, concat_axis=0, tiled=True)  4.28 us
  transfers between devices with their start and end apart: 27, of which 15 were waited for; matrix products, arithmetic and copies ran while one was open for 5% of the time, Pallas kernels for 7%

profile of v3, /device:TPU:32, one launch (start us, length us, event | category | flops | bytes accessed | tf_op | source)
XLA Modules:
  0.0 181.3 jit_solution(10454470138313352148)
XLA Ops:
  6.5 1.6 copy.14
  8.2 0.4 subtract_convert_fusion
  8.6 0.0 copy-start.3
  8.6 1.1 pad_maximum_fusion
  9.8 0.0 all-gather.3.cloned.1.call-update
  9.8 2.0 %collective-permute-start = (bf16[896,128]{1,0:T(8,128)(2,1)S(1)}, bf16[896,128]{1,0:T(8,128)(2,1)S(1)}, u32[]{:S(2)}, u32[]{:S(2)}) collective-permute-start(bf16[896,128]{1,0:T(8,128)(2,1)S(1)} %get-tuple-element.24), channel_id=1, source_target_pairs={{0,32},{8,40},{16,48},{24,56},{32,64},{40,72},{48,80},{56,88},{64,... | collective-permute-start | bytes 688136 | tf_op jit(solution)/shard_map/other_z_up1/ppermute | solution.py:22
  11.8 0.1 collective-permute-start.7
  11.9 1.5 collective-permute-start.4
  13.4 1.7 collective-permute-start.5
  15.2 1.8 collective-permute-start.6
  17.0 0.3 collective-permute-done
  17.3 1.9 %collective-permute-start.1 = (bf16[896,128]{1,0:T(8,128)(2,1)S(1)}, bf16[896,128]{1,0:T(8,128)(2,1)S(1)}, u32[]{:S(2)}, u32[]{:S(2)}) collective-permute-start(bf16[896,128]{1,0:T(8,128)(2,1)S(1)} %collective-permute-done), channel_id=1, source_target_pairs={{0,32},{8,40},{16,48},{24,56},{32,64},{40,72},{48,80},{56,88},{64,... | collective-permute-start | bytes 688136 | tf_op jit(solution)/shard_map/other_z_up2/ppermute | solution.py:22
  19.2 2.3 %collective-permute-start.8 = (bf16[896,128]{1,0:T(8,128)(2,1)S(1)}, bf16[896,128]{1,0:T(8,128)(2,1)S(1)}, u32[]{:S(2)}, u32[]{:S(2)}) collective-permute-start(bf16[896,128]{1,0:T(8,128)(2,1)S(1)} %collective-permute-done.7), channel_id=1, source_target_pairs={{0,224},{8,232},{16,240},{24,248},{32,0},{40,8},{48,16},{56,24},{6... | collective-permute-start | bytes 688136 | tf_op jit(solution)/shard_map/other_z_down2/ppermute | solution.py:22
  21.5 2.8 %collective-permute-done.5 = bf16[896,128]{1,0:T(8,128)(2,1)S(1)} collective-permute-done((bf16[896,128]{1,0:T(8,128)(2,1)S(1)}, bf16[896,128]{1,0:T(8,128)(2,1)S(1)}, u32[]{:S(2)}, u32[]{:S(2)}) %collective-permute-start.5) | collective-permute-done | bytes 229408 | tf_op jit(solution)/shard_map/first_x_down/ppermute | solution.py:25
  24.3 1.7 collective-permute-done.6
  26.0 0.1 pad_maximum_fusion.1.refs_0_
  26.1 0.4 collective-permute-done.1
  26.5 1.6 collective-permute-start.2
  28.1 2.3 %collective-permute-start.9 = (bf16[896,128]{1,0:T(8,128)(2,1)S(1)}, bf16[896,128]{1,0:T(8,128)(2,1)S(1)}, u32[]{:S(2)}, u32[]{:S(2)}) collective-permute-start(bf16[896,128]{1,0:T(8,128)(2,1)S(1)} %collective-permute-done.8), channel_id=1, source_target_pairs={{0,224},{8,232},{16,240},{24,248},{32,0},{40,8},{48,16},{56,24},{6... | collective-permute-start | bytes 688136 | tf_op jit(solution)/shard_map/other_z_down3/ppermute | solution.py:22
  30.4 0.1 pad_maximum_fusion.2.refs_0_
  30.5 1.2 collective-permute-start.13
  31.7 3.0 %collective-permute-done.2 = bf16[896,128]{1,0:T(8,128)(2,1)S(1)} collective-permute-done((bf16[896,128]{1,0:T(8,128)(2,1)S(1)}, bf16[896,128]{1,0:T(8,128)(2,1)S(1)}, u32[]{:S(2)}, u32[]{:S(2)}) %collective-permute-start.2) | collective-permute-done | bytes 229408 | tf_op jit(solution)/shard_map/other_z_up3/ppermute | solution.py:22
  34.7 0.2 collective-permute-start.3
  35.0 0.4 collective-permute-done.9
  35.4 2.5 %collective-permute-start.10 = (bf16[448,128]{1,0:T(8,128)(2,1)S(1)}, bf16[448,128]{1,0:T(8,128)(2,1)S(1)}, u32[]{:S(2)}, u32[]{:S(2)}) collective-permute-start(bf16[448,128]{1,0:T(8,128)(2,1)S(1)} %slice.40), channel_id=1, source_target_pairs={{0,224},{8,232},{16,240},{24,248},{32,0},{40,8},{48,16},{56,24},{6... | collective-permute-start | bytes 344072 | tf_op jit(solution)/shard_map/other_z_down_last/ppermute | solution.py:22
  38.0 2.6 %collective-permute-done.3 = bf16[448,128]{1,0:T(8,128)(2,1)S(1)} collective-permute-done((bf16[448,128]{1,0:T(8,128)(2,1)S(1)}, bf16[448,128]{1,0:T(8,128)(2,1)S(1)}, u32[]{:S(2)}, u32[]{:S(2)}) %collective-permute-start.3) | collective-permute-done | bytes 114720 | tf_op jit(solution)/shard_map/other_z_up_last/ppermute | solution.py:22
  40.6 0.5 collective-permute-done.10
  41.1 2.1 %collective-permute-start.14 = (bf16[3584,128]{1,0:T(8,128)(2,1)S(1)}, bf16[3584,128]{1,0:T(8,128)(2,1)S(1)}, u32[]{:S(2)}, u32[]{:S(2)}) collective-permute-start(bf16[3584,128]{1,0:T(8,128)(2,1)S(1)} %constant_dynamic-update-slice_fusion.refs_1_), channel_id=1, source_target_pairs={{0,24},{8,0},{16,8},{24,16},{32,56},{40,32},{48,40},{56,48},{64,88... | collective-permute-start | bytes 2752520 | tf_op jit(solution)/shard_map/other_x_down1_two/ppermute | solution.py:25
  43.1 2.6 %collective-permute-start.12 = (bf16[3584,128]{1,0:T(8,128)(2,1)S(1)}, bf16[3584,128]{1,0:T(8,128)(2,1)S(1)}, u32[]{:S(2)}, u32[]{:S(2)}) collective-permute-start(bf16[3584,128]{1,0:T(8,128)(2,1)S(1)} %pad_maximum_fusion.1.refs_0_), channel_id=1, source_target_pairs={{0,224},{8,232},{16,240},{24,248},{32,0},{40,8},{48,16},{56,24},{6... | collective-permute-start | bytes 2752520 | tf_op jit(solution)/shard_map/first_z_down1/ppermute | solution.py:22
  45.8 0.7 collective-permute-start.11
  46.5 0.5 collective-permute-start.18
  47.0 5.4 %collective-permute-done.13.refs_2_ = bf16[3584,128]{1,0:T(8,128)(2,1)S(1)} collective-permute-done((bf16[3584,128]{1,0:T(8,128)(2,1)S(1)}, bf16[3584,128]{1,0:T(8,128)(2,1)S(1)}, u32[]{:S(2)}, u32[]{:S(2)}) %collective-permute-start.13) | collective-permute-done | bytes 917536 | tf_op jit(solution)/shard_map/other_x_up1_one/ppermute | solution.py:25
  52.4 12.0 %collective-permute-done.14.refs_3_ = bf16[3584,128]{1,0:T(8,128)(2,1)S(1)} collective-permute-done((bf16[3584,128]{1,0:T(8,128)(2,1)S(1)}, bf16[3584,128]{1,0:T(8,128)(2,1)S(1)}, u32[]{:S(2)}, u32[]{:S(2)}) %collective-permute-start.14) | collective-permute-done | bytes 917536 | tf_op jit(solution)/shard_map/other_x_down1_two/ppermute | solution.py:25
  64.4 2.8 %collective-permute-start.16 = (bf16[3584,128]{1,0:T(8,128)(2,1)S(1)}, bf16[3584,128]{1,0:T(8,128)(2,1)}, u32[]{:S(2)}, u32[]{:S(2)}) collective-permute-start(bf16[3584,128]{1,0:T(8,128)(2,1)S(1)} %collective-permute-done.12.refs_2_), channel_id=1, source_target_pairs={{0,224},{8,232},{16,240},{24,248},{32,0},{40,8},{48,16},{56,24},{6... | collective-permute-start | bytes 2752520 | tf_op jit(solution)/shard_map/first_z_down2/ppermute | solution.py:22
  67.3 0.7 collective-permute-start.15
  68.0 12.2 %collective-permute-done.18.refs_5_ = bf16[3584,128]{1,0:T(8,128)(2,1)S(1)} collective-permute-done((bf16[3584,128]{1,0:T(8,128)(2,1)S(1)}, bf16[3584,128]{1,0:T(8,128)(2,1)S(1)}, u32[]{:S(2)}, u32[]{:S(2)}) %collective-permute-start.18) | collective-permute-done | bytes 917536 | tf_op jit(solution)/shard_map/other_x_down1_one/ppermute | solution.py:25
  80.2 4.6 %collective-permute-done.16.refs_4_ = bf16[3584,128]{1,0:T(8,128)(2,1)} collective-permute-done((bf16[3584,128]{1,0:T(8,128)(2,1)S(1)}, bf16[3584,128]{1,0:T(8,128)(2,1)}, u32[]{:S(2)}, u32[]{:S(2)}) %collective-permute-start.16) | collective-permute-done | bytes 917536 | tf_op jit(solution)/shard_map/first_z_down2/ppermute | solution.py:22
  84.8 2.2 %collective-permute-start.20 = (bf16[3584,128]{1,0:T(8,128)(2,1)}, bf16[3584,128]{1,0:T(8,128)(2,1)S(1)}, u32[]{:S(2)}, u32[]{:S(2)}) collective-permute-start(bf16[3584,128]{1,0:T(8,128)(2,1)} %collective-permute-done.16.refs_4_), channel_id=1, source_target_pairs={{0,224},{8,232},{16,240},{24,248},{32,0},{40,8},{48,16},{56,24},{6... | collective-permute-start | bytes 2752520 | tf_op jit(solution)/shard_map/first_z_down3/ppermute | solution.py:22
  87.1 0.5 collective-permute-done.15.refs_3_
  87.5 0.7 collective-permute-start.19
  88.2 0.1 select_reduce_fusion
  88.3 0.7 collective-permute-start.23
  89.0 2.6 %collective-permute-start.24 = (bf16[3584,128]{1,0:T(8,128)(2,1)}, bf16[3584,128]{1,0:T(8,128)(2,1)}, u32[]{:S(2)}, u32[]{:S(2)}) collective-permute-start(bf16[3584,128]{1,0:T(8,128)(2,1)} %copy-done.11), channel_id=1, source_target_pairs={{0,24},{8,0},{16,8},{24,16},{32,56},{40,32},{48,40},{56,48},{64,88... | collective-permute-start | bytes 2752520 | tf_op jit(solution)/shard_map/other_x_down_last/ppermute | solution.py:25
  91.7 0.6 pad_add_fusion.place_ref
  92.2 0.1 fusion.9
  92.3 5.6 %copy.15 = bf16[896,1792]{0,1:T(8,128)(2,1)} copy(bf16[896,1792]{1,0:T(8,128)(2,1)} %param.10) | data formatting | bytes 6422528 | tf_op jit(solution)/shard_map/optimization_barrier | solution.py:62
  97.9 7.5 %collective-permute-done.20.refs_6_ = bf16[3584,128]{1,0:T(8,128)(2,1)S(1)} collective-permute-done((bf16[3584,128]{1,0:T(8,128)(2,1)}, bf16[3584,128]{1,0:T(8,128)(2,1)S(1)}, u32[]{:S(2)}, u32[]{:S(2)}) %collective-permute-start.20) | collective-permute-done | bytes 917536 | tf_op jit(solution)/shard_map/first_z_down3/ppermute | solution.py:22
  105.4 2.5 %collective-permute-start.22 = (bf16[1792,128]{1,0:T(8,128)(2,1)S(1)}, bf16[1792,128]{1,0:T(8,128)(2,1)S(1)}, u32[]{:S(2)}, u32[]{:S(2)}) collective-permute-start(bf16[1792,128]{1,0:T(8,128)(2,1)S(1)} %slice.42), channel_id=1, source_target_pairs={{0,224},{8,232},{16,240},{24,248},{32,0},{40,8},{48,16},{56,24},{6... | collective-permute-start | bytes 1376264 | tf_op jit(solution)/shard_map/first_z_down_last/ppermute | solution.py:22
  107.9 1.0 slice.41
  109.0 1.4 collective-permute-start.21
  110.3 1.8 convert_reduce_fusion
  112.2 12.6 %shard_map.83 = f32[64,896]{1,0:T(8,128)} custom-call(s32[4]{0:T(128)} %pad_add_fusion.place_ref, bf16[8,640,896]{2,1,0:T(8,128)(2,1)} %bitcast.26, bf16[1792,896]{1,0:T(8,128)(2,1)} %bitcast.23, bf16[64,1792]{1,0:T(8,128)(2,1)} %bitcast.28, bf16[3584,128]{1,0:T(8,128)(2,1)} %copy-done.2, bf16[3584,128]{1,0:T(8,128)(2,1)} %copy-done.7, ...), custom_call_target="tpu_custom_call" | custom-call | flops 6987710464 | bytes 16285696 | tf_op jit(solution)/shard_map/pallas_call | solution.py:155
  124.8 0.8 copy-done.14
  125.6 12.5 %shard_map.82 = f32[64,896]{1,0:T(8,128)} custom-call(s32[4]{0:T(128)} %pad_add_fusion.place_ref, bf16[8,640,896]{2,1,0:T(8,128)(2,1)} %bitcast.27, bf16[1792,896]{1,0:T(8,128)(2,1)} %bitcast.24, bf16[64,1792]{1,0:T(8,128)(2,1)} %bitcast.29, bf16[3584,128]{1,0:T(8,128)(2,1)} %copy-done.1, bf16[3584,128]{1,0:T(8,128)(2,1)} %copy-done.10, ...), custom_call_target="tpu_custom_call" | custom-call | flops 6987710464 | bytes 16285696 | tf_op jit(solution)/shard_map/pallas_call | solution.py:155
  138.2 0.0 copy-start.15
  138.2 2.6 %fusion = f32[8,64,64]{2,1,0:T(8,128)S(1)} fusion(f32[64,896]{1,0:T(8,128)S(1)} %slice_add_fusion, f32[8,896]{1,0:T(8,128)S(1)} %fusion.9, f32[64,896]{1,0:T(8,128)} %shard_map.82, f32[64,896]{1,0:T(8,128)S(1)} %copy-done.5), kind=kOutput, calls=%fused_computation.1 | convolution fusion | flops 352837632 | bytes 847872 | tf_op jit(solution)/shard_map/cpt,qt->cpq/dot_general | solution.py:238
  140.8 0.1 reshape.75
  140.9 0.7 copy.18
  141.6 4.3 %all-to-all-start = ((f32[8,8,512]{2,1,0:T(8,128)}), f32[8,8,512]{2,1,0:T(8,128)S(1)}, u32[]{:S(2)}, u32[]{:S(2)}) async-start(f32[8,8,512]{2,1,0:T(8,128)} %bitcast.21), calls=%async_computation | async-start | bytes 262144 | tf_op jit(solution)/shard_map/all_to_all | solution.py:240
  145.9 0.1 dynamic_slice.3
  146.0 6.1 %all-to-all-done = f32[8,8,512]{2,1,0:T(8,128)S(1)} async-done(((f32[8,8,512]{2,1,0:T(8,128)}), f32[8,8,512]{2,1,0:T(8,128)S(1)}, u32[]{:S(2)}, u32[]{:S(2)}) %all-to-all-start) | async-done | bytes 131104 | tf_op jit(solution)/shard_map/all_to_all | solution.py:240
  152.0 0.2 fusion.2
  152.3 21.4 %all_to_all.14 = bf16[32,8,512]{2,1,0:T(8,128)(2,1)S(1)} all-to-all(bf16[32,8,512]{2,1,0:T(8,128)(2,1)S(1)} %fusion.2), channel_id=1, replica_groups=mesh['dp'=32,'tensor'=8] {'dp'}, dimensions={0} | all-to-all | bytes 524288 | tf_op jit(solution)/shard_map/all_to_all | solution.py:193
  173.7 0.7 reshape.76
  (59 shorter events, 0.4 us)
Async XLA Ops:
  6.5 1.6 copy-start
  6.5 1.6 copy-start.6
  6.5 103.8 %all-gather.3.cloned.1.call-start = ((), (), s32[]{:S(2)}) async-start(), calls=%async_computation.2 | async-start | bytes 10321920 | tf_op jit(solution)/shard_map/all_gather | solution.py:226
  8.6 1.2 copy-start.3
  9.8 7.4 %collective-permute-start = (bf16[896,128]{1,0:T(8,128)(2,1)S(1)}, bf16[896,128]{1,0:T(8,128)(2,1)S(1)}, u32[]{:S(2)}, u32[]{:S(2)}) collective-permute-start(bf16[896,128]{1,0:T(8,128)(2,1)S(1)} %get-tuple-element.24), channel_id=1, source_target_pairs={{0,32},{8,40},{16,48},{24,56},{32,64},{40,72},{48,80},{56,88},{64,... | collective-permute-start | bytes 688136 | tf_op jit(solution)/shard_map/other_z_up1/ppermute | solution.py:22
  11.8 7.3 %collective-permute-start.7 = (bf16[896,128]{1,0:T(8,128)(2,1)S(1)}, bf16[896,128]{1,0:T(8,128)(2,1)S(1)}, u32[]{:S(2)}, u32[]{:S(2)}) collective-permute-start(bf16[896,128]{1,0:T(8,128)(2,1)S(1)} %get-tuple-element.24), channel_id=1, source_target_pairs={{0,224},{8,232},{16,240},{24,248},{32,0},{40,8},{48,16},{56,24},{6... | collective-permute-start | bytes 688136 | tf_op jit(solution)/shard_map/other_z_down1/ppermute | solution.py:22
  11.9 9.5 %collective-permute-start.4 = (bf16[896,128]{1,0:T(8,128)(2,1)S(1)}, bf16[896,128]{1,0:T(8,128)(2,1)S(1)}, u32[]{:S(2)}, u32[]{:S(2)}) collective-permute-start(bf16[896,128]{1,0:T(8,128)(2,1)S(1)} %get-tuple-element.23), channel_id=1, source_target_pairs={{0,8},{8,16},{16,24},{24,0},{32,40},{40,48},{48,56},{56,32},{64,72... | collective-permute-start | bytes 688136 | tf_op jit(solution)/shard_map/first_x_up/ppermute | solution.py:25
  13.4 10.9 %collective-permute-start.5 = (bf16[896,128]{1,0:T(8,128)(2,1)S(1)}, bf16[896,128]{1,0:T(8,128)(2,1)S(1)}, u32[]{:S(2)}, u32[]{:S(2)}) collective-permute-start(bf16[896,128]{1,0:T(8,128)(2,1)S(1)} %get-tuple-element.23), channel_id=1, source_target_pairs={{0,24},{8,0},{16,8},{24,16},{32,56},{40,32},{48,40},{56,48},{64,88... | collective-permute-start | bytes 688136 | tf_op jit(solution)/shard_map/first_x_down/ppermute | solution.py:25
  15.2 10.8 %collective-permute-start.6 = (bf16[896,128]{1,0:T(8,128)(2,1)S(1)}, bf16[896,128]{1,0:T(8,128)(2,1)S(1)}, u32[]{:S(2)}, u32[]{:S(2)}) collective-permute-start(bf16[896,128]{1,0:T(8,128)(2,1)S(1)} %get-tuple-element.23), channel_id=1, source_target_pairs={{0,16},{8,24},{16,0},{24,8},{32,48},{40,56},{48,32},{56,40},{64,80... | collective-permute-start | bytes 688136 | tf_op jit(solution)/shard_map/first_x_far/ppermute | solution.py:25
  17.3 9.3 %collective-permute-start.1 = (bf16[896,128]{1,0:T(8,128)(2,1)S(1)}, bf16[896,128]{1,0:T(8,128)(2,1)S(1)}, u32[]{:S(2)}, u32[]{:S(2)}) collective-permute-start(bf16[896,128]{1,0:T(8,128)(2,1)S(1)} %collective-permute-done), channel_id=1, source_target_pairs={{0,32},{8,40},{16,48},{24,56},{32,64},{40,72},{48,80},{56,88},{64,... | collective-permute-start | bytes 688136 | tf_op jit(solution)/shard_map/other_z_up2/ppermute | solution.py:22
  19.2 8.9 %collective-permute-start.8 = (bf16[896,128]{1,0:T(8,128)(2,1)S(1)}, bf16[896,128]{1,0:T(8,128)(2,1)S(1)}, u32[]{:S(2)}, u32[]{:S(2)}) collective-permute-start(bf16[896,128]{1,0:T(8,128)(2,1)S(1)} %collective-permute-done.7), channel_id=1, source_target_pairs={{0,224},{8,232},{16,240},{24,248},{32,0},{40,8},{48,16},{56,24},{6... | collective-permute-start | bytes 688136 | tf_op jit(solution)/shard_map/other_z_down2/ppermute | solution.py:22
  26.1 19.7 %copy-start.1 = (bf16[3584,128]{1,0:T(8,128)(2,1)}, bf16[3584,128]{1,0:T(8,128)(2,1)S(1)}, u32[]{:S(2)}) copy-start(bf16[3584,128]{1,0:T(8,128)(2,1)S(1)} %pad_maximum_fusion.1.refs_0_) | copy-start | bytes 2752516
  26.1 62.1 %copy-start.16 = (s32[1,8]{1,0:T(1,128)S(1)}, s32[1,8]{1,0:T(1,128)}, u32[]{:S(2)}) copy-start(s32[1,8]{1,0:T(1,128)} %param.14) | copy-start | bytes 100
  26.5 8.2 %collective-permute-start.2 = (bf16[896,128]{1,0:T(8,128)(2,1)S(1)}, bf16[896,128]{1,0:T(8,128)(2,1)S(1)}, u32[]{:S(2)}, u32[]{:S(2)}) collective-permute-start(bf16[896,128]{1,0:T(8,128)(2,1)S(1)} %collective-permute-done.1), channel_id=1, source_target_pairs={{0,32},{8,40},{16,48},{24,56},{32,64},{40,72},{48,80},{56,88},{64,... | collective-permute-start | bytes 688136 | tf_op jit(solution)/shard_map/other_z_up3/ppermute | solution.py:22
  28.1 7.3 %collective-permute-start.9 = (bf16[896,128]{1,0:T(8,128)(2,1)S(1)}, bf16[896,128]{1,0:T(8,128)(2,1)S(1)}, u32[]{:S(2)}, u32[]{:S(2)}) collective-permute-start(bf16[896,128]{1,0:T(8,128)(2,1)S(1)} %collective-permute-done.8), channel_id=1, source_target_pairs={{0,224},{8,232},{16,240},{24,248},{32,0},{40,8},{48,16},{56,24},{6... | collective-permute-start | bytes 688136 | tf_op jit(solution)/shard_map/other_z_down3/ppermute | solution.py:22
  30.5 67.4 %copy-start.2 = (bf16[3584,128]{1,0:T(8,128)(2,1)}, bf16[3584,128]{1,0:T(8,128)(2,1)S(1)}, u32[]{:S(2)}) copy-start(bf16[3584,128]{1,0:T(8,128)(2,1)S(1)} %pad_maximum_fusion.2.refs_0_) | copy-start | bytes 2752516
  30.5 21.9 %collective-permute-start.13 = (bf16[3584,128]{1,0:T(8,128)(2,1)S(1)}, bf16[3584,128]{1,0:T(8,128)(2,1)S(1)}, u32[]{:S(2)}, u32[]{:S(2)}) collective-permute-start(bf16[3584,128]{1,0:T(8,128)(2,1)S(1)} %pad_maximum_fusion.2.refs_0_), channel_id=1, source_target_pairs={{0,8},{8,16},{16,24},{24,0},{32,40},{40,48},{48,56},{56,32},{64,72... | collective-permute-start | bytes 2752520 | tf_op jit(solution)/shard_map/other_x_up1_one/ppermute | solution.py:25
  34.7 5.8 %collective-permute-start.3 = (bf16[448,128]{1,0:T(8,128)(2,1)S(1)}, bf16[448,128]{1,0:T(8,128)(2,1)S(1)}, u32[]{:S(2)}, u32[]{:S(2)}) collective-permute-start(bf16[448,128]{1,0:T(8,128)(2,1)S(1)} %slice.39), channel_id=1, source_target_pairs={{0,32},{8,40},{16,48},{24,56},{32,64},{40,72},{48,80},{56,88},{64,... | collective-permute-start | bytes 344072 | tf_op jit(solution)/shard_map/other_z_up_last/ppermute | solution.py:22
  35.4 5.7 %collective-permute-start.10 = (bf16[448,128]{1,0:T(8,128)(2,1)S(1)}, bf16[448,128]{1,0:T(8,128)(2,1)S(1)}, u32[]{:S(2)}, u32[]{:S(2)}) collective-permute-start(bf16[448,128]{1,0:T(8,128)(2,1)S(1)} %slice.40), channel_id=1, source_target_pairs={{0,224},{8,232},{16,240},{24,248},{32,0},{40,8},{48,16},{56,24},{6... | collective-permute-start | bytes 344072 | tf_op jit(solution)/shard_map/other_z_down_last/ppermute | solution.py:22
  41.1 39.1 %copy-start.7 = (bf16[3584,128]{1,0:T(8,128)(2,1)}, bf16[3584,128]{1,0:T(8,128)(2,1)S(1)}, u32[]{:S(2)}) copy-start(bf16[3584,128]{1,0:T(8,128)(2,1)S(1)} %constant_dynamic-update-slice_fusion.refs_1_) | copy-start | bytes 2752516
  41.1 23.4 %collective-permute-start.14 = (bf16[3584,128]{1,0:T(8,128)(2,1)S(1)}, bf16[3584,128]{1,0:T(8,128)(2,1)S(1)}, u32[]{:S(2)}, u32[]{:S(2)}) collective-permute-start(bf16[3584,128]{1,0:T(8,128)(2,1)S(1)} %constant_dynamic-update-slice_fusion.refs_1_), channel_id=1, source_target_pairs={{0,24},{8,0},{16,8},{24,16},{32,56},{40,32},{48,40},{56,48},{64,88... | collective-permute-start | bytes 2752520 | tf_op jit(solution)/shard_map/other_x_down1_two/ppermute | solution.py:25
  43.1 21.3 %collective-permute-start.12 = (bf16[3584,128]{1,0:T(8,128)(2,1)S(1)}, bf16[3584,128]{1,0:T(8,128)(2,1)S(1)}, u32[]{:S(2)}, u32[]{:S(2)}) collective-permute-start(bf16[3584,128]{1,0:T(8,128)(2,1)S(1)} %pad_maximum_fusion.1.refs_0_), channel_id=1, source_target_pairs={{0,224},{8,232},{16,240},{24,248},{32,0},{40,8},{48,16},{56,24},{6... | collective-permute-start | bytes 2752520 | tf_op jit(solution)/shard_map/first_z_down1/ppermute | solution.py:22
  45.8 21.5 %collective-permute-start.11 = (bf16[3584,128]{1,0:T(8,128)(2,1)S(1)}, bf16[3584,128]{1,0:T(8,128)(2,1)S(1)}, u32[]{:S(2)}, u32[]{:S(2)}) collective-permute-start(bf16[3584,128]{1,0:T(8,128)(2,1)S(1)} %pad_maximum_fusion.1.refs_0_), channel_id=1, source_target_pairs={{0,32},{8,40},{16,48},{24,56},{32,64},{40,72},{48,80},{56,88},{64,... | collective-permute-start | bytes 2752520 | tf_op jit(solution)/shard_map/first_z_up1/ppermute | solution.py:22
  46.5 33.7 %collective-permute-start.18 = (bf16[3584,128]{1,0:T(8,128)(2,1)S(1)}, bf16[3584,128]{1,0:T(8,128)(2,1)S(1)}, u32[]{:S(2)}, u32[]{:S(2)}) collective-permute-start(bf16[3584,128]{1,0:T(8,128)(2,1)S(1)} %pad_maximum_fusion.2.refs_0_), channel_id=1, source_target_pairs={{0,24},{8,0},{16,8},{24,16},{32,56},{40,32},{48,40},{56,48},{64,88... | collective-permute-start | bytes 2752520 | tf_op jit(solution)/shard_map/other_x_down1_one/ppermute | solution.py:25
  52.4 32.5 %copy-start.8 = (bf16[3584,128]{1,0:T(8,128)(2,1)}, bf16[3584,128]{1,0:T(8,128)(2,1)S(1)}, u32[]{:S(2)}) copy-start(bf16[3584,128]{1,0:T(8,128)(2,1)S(1)} %collective-permute-done.13.refs_2_) | copy-start | bytes 2752516
  52.4 27.8 %collective-permute-start.17 = (bf16[3584,128]{1,0:T(8,128)(2,1)S(1)}, bf16[3584,128]{1,0:T(8,128)(2,1)S(1)}, u32[]{:S(2)}, u32[]{:S(2)}) collective-permute-start(bf16[3584,128]{1,0:T(8,128)(2,1)S(1)} %constant_dynamic-update-slice_fusion.refs_1_), channel_id=1, source_target_pairs={{0,8},{8,16},{16,24},{24,0},{32,40},{40,48},{48,56},{56,32},{64,72... | collective-permute-start | bytes 2752520 | tf_op jit(solution)/shard_map/other_x_up1_two/ppermute | solution.py:25
  64.4 23.8 %copy-start.11 = (bf16[3584,128]{1,0:T(8,128)(2,1)}, bf16[3584,128]{1,0:T(8,128)(2,1)S(1)}, u32[]{:S(2)}) copy-start(bf16[3584,128]{1,0:T(8,128)(2,1)S(1)} %collective-permute-done.14.refs_3_) | copy-start | bytes 2752516
  64.4 22.6 %copy-start.9 = (bf16[3584,128]{1,0:T(8,128)(2,1)}, bf16[3584,128]{1,0:T(8,128)(2,1)S(1)}, u32[]{:S(2)}) copy-start(bf16[3584,128]{1,0:T(8,128)(2,1)S(1)} %collective-permute-done.12.refs_2_) | copy-start | bytes 2752516
  64.4 20.4 %collective-permute-start.16 = (bf16[3584,128]{1,0:T(8,128)(2,1)S(1)}, bf16[3584,128]{1,0:T(8,128)(2,1)}, u32[]{:S(2)}, u32[]{:S(2)}) collective-permute-start(bf16[3584,128]{1,0:T(8,128)(2,1)S(1)} %collective-permute-done.12.refs_2_), channel_id=1, source_target_pairs={{0,224},{8,232},{16,240},{24,248},{32,0},{40,8},{48,16},{56,24},{6... | collective-permute-start | bytes 2752520 | tf_op jit(solution)/shard_map/first_z_down2/ppermute | solution.py:22
  67.3 20.2 %copy-start.10 = (bf16[3584,128]{1,0:T(8,128)(2,1)}, bf16[3584,128]{1,0:T(8,128)(2,1)S(1)}, u32[]{:S(2)}) copy-start(bf16[3584,128]{1,0:T(8,128)(2,1)S(1)} %collective-permute-done.11.refs_1_) | copy-start | bytes 2752516
  67.3 20.2 %collective-permute-start.15 = (bf16[3584,128]{1,0:T(8,128)(2,1)S(1)}, bf16[3584,128]{1,0:T(8,128)(2,1)}, u32[]{:S(2)}, u32[]{:S(2)}) collective-permute-start(bf16[3584,128]{1,0:T(8,128)(2,1)S(1)} %collective-permute-done.11.refs_1_), channel_id=1, source_target_pairs={{0,32},{8,40},{16,48},{24,56},{32,64},{40,72},{48,80},{56,88},{64,... | collective-permute-start | bytes 2752520 | tf_op jit(solution)/shard_map/first_z_up2/ppermute | solution.py:22
  80.2 8.0 %copy-start.12 = (bf16[3584,128]{1,0:T(8,128)(2,1)}, bf16[3584,128]{1,0:T(8,128)(2,1)S(1)}, u32[]{:S(2)}) copy-start(bf16[3584,128]{1,0:T(8,128)(2,1)S(1)} %collective-permute-done.18.refs_5_) | copy-start | bytes 2752516
  80.2 8.0 %copy-start.13 = (bf16[3584,128]{1,0:T(8,128)(2,1)}, bf16[3584,128]{1,0:T(8,128)(2,1)S(1)}, u32[]{:S(2)}) copy-start(bf16[3584,128]{1,0:T(8,128)(2,1)S(1)} %collective-permute-done.17.refs_4_) | copy-start | bytes 2752516
  84.8 20.5 %collective-permute-start.20 = (bf16[3584,128]{1,0:T(8,128)(2,1)}, bf16[3584,128]{1,0:T(8,128)(2,1)S(1)}, u32[]{:S(2)}, u32[]{:S(2)}) collective-permute-start(bf16[3584,128]{1,0:T(8,128)(2,1)} %collective-permute-done.16.refs_4_), channel_id=1, source_target_pairs={{0,224},{8,232},{16,240},{24,248},{32,0},{40,8},{48,16},{56,24},{6... | collective-permute-start | bytes 2752520 | tf_op jit(solution)/shard_map/first_z_down3/ppermute | solution.py:22
  87.5 20.4 %collective-permute-start.19 = (bf16[3584,128]{1,0:T(8,128)(2,1)}, bf16[3584,128]{1,0:T(8,128)(2,1)}, u32[]{:S(2)}, u32[]{:S(2)}) collective-permute-start(bf16[3584,128]{1,0:T(8,128)(2,1)} %collective-permute-done.15.refs_3_), channel_id=1, source_target_pairs={{0,32},{8,40},{16,48},{24,56},{32,64},{40,72},{48,80},{56,88},{64,... | collective-permute-start | bytes 2752520 | tf_op jit(solution)/shard_map/first_z_up3/ppermute | solution.py:22
  88.3 23.8 %collective-permute-start.23 = (bf16[3584,128]{1,0:T(8,128)(2,1)}, bf16[3584,128]{1,0:T(8,128)(2,1)}, u32[]{:S(2)}, u32[]{:S(2)}) collective-permute-start(bf16[3584,128]{1,0:T(8,128)(2,1)} %copy-done.8), channel_id=1, source_target_pairs={{0,8},{8,16},{16,24},{24,0},{32,40},{40,48},{48,56},{56,32},{64,72... | collective-permute-start | bytes 2752520 | tf_op jit(solution)/shard_map/other_x_up_last/ppermute | solution.py:25
  89.0 23.1 %collective-permute-start.24 = (bf16[3584,128]{1,0:T(8,128)(2,1)}, bf16[3584,128]{1,0:T(8,128)(2,1)}, u32[]{:S(2)}, u32[]{:S(2)}) collective-permute-start(bf16[3584,128]{1,0:T(8,128)(2,1)} %copy-done.11), channel_id=1, source_target_pairs={{0,24},{8,0},{16,8},{24,16},{32,56},{40,32},{48,40},{56,48},{64,88... | collective-permute-start | bytes 2752520 | tf_op jit(solution)/shard_map/other_x_down_last/ppermute | solution.py:25
  105.4 6.7 %copy-start.4 = (bf16[3584,128]{1,0:T(8,128)(2,1)}, bf16[3584,128]{1,0:T(8,128)(2,1)S(1)}, u32[]{:S(2)}) copy-start(bf16[3584,128]{1,0:T(8,128)(2,1)S(1)} %collective-permute-done.20.refs_6_) | copy-start | bytes 2752516
  105.4 19.4 %collective-permute-start.22 = (bf16[1792,128]{1,0:T(8,128)(2,1)S(1)}, bf16[1792,128]{1,0:T(8,128)(2,1)S(1)}, u32[]{:S(2)}, u32[]{:S(2)}) collective-permute-start(bf16[1792,128]{1,0:T(8,128)(2,1)S(1)} %slice.42), channel_id=1, source_target_pairs={{0,224},{8,232},{16,240},{24,248},{32,0},{40,8},{48,16},{56,24},{6... | collective-permute-start | bytes 1376264 | tf_op jit(solution)/shard_map/first_z_down_last/ppermute | solution.py:22
  109.0 15.9 %collective-permute-start.21 = (bf16[1792,128]{1,0:T(8,128)(2,1)S(1)}, bf16[1792,128]{1,0:T(8,128)(2,1)}, u32[]{:S(2)}, u32[]{:S(2)}) collective-permute-start(bf16[1792,128]{1,0:T(8,128)(2,1)S(1)} %slice.41), channel_id=1, source_target_pairs={{0,32},{8,40},{16,48},{24,56},{32,64},{40,72},{48,80},{56,88},{64,... | collective-permute-start | bytes 1376264 | tf_op jit(solution)/shard_map/first_z_up_last/ppermute | solution.py:22
  124.8 13.4 %copy-start.5 = (f32[64,896]{1,0:T(8,128)S(1)}, f32[64,896]{1,0:T(8,128)}, u32[]{:S(2)}) copy-start(f32[64,896]{1,0:T(8,128)} %shard_map.83) | copy-start | bytes 688132
  124.8 0.8 copy-start.14
  138.2 7.7 %copy-start.15 = (s32[256]{0:T(256)S(1)}, s32[256]{0:T(256)}, u32[]{:S(2)}) copy-start(s32[256]{0:T(256)} %param.15) | copy-start | bytes 3076
  141.6 10.4 %all-to-all-start = ((f32[8,8,512]{2,1,0:T(8,128)}), f32[8,8,512]{2,1,0:T(8,128)S(1)}, u32[]{:S(2)}, u32[]{:S(2)}) async-start(f32[8,8,512]{2,1,0:T(8,128)} %bitcast.21), calls=%async_computation | async-start | bytes 262144 | tf_op jit(solution)/shard_map/all_to_all | solution.py:240
Sparse Core Ops, SparseCore 0:
  9.9 58.1 all-gather.2

commit v4 on v3

--- a/solution.py
+++ b/solution.py
@@ -203,18 +203,19 @@
     group, shard = lax.axis_index("dp"), lax.axis_index("tensor")
     place = jnp.stack([group // NX, group % NX, shard // NC, shard % NC]).astype(jnp.int32)
 
-    in_part = jnp.dot(activations, proj_in, preferred_element_type=jnp.float32)
-    in_high = in_part.astype(jnp.bfloat16)
-    in_low = (in_part - in_high.astype(jnp.float32)).astype(jnp.bfloat16)
-    own = jnp.concatenate([out_grads.T, in_high.T, in_low.T], axis=0)
-    own = with_layout_constraint(own, Layout(major_to_minor=(0, 1)))
-
     rows = w_down.shape[0]
     first = Blocks(w_down[:FIRST], [(0, 0, 0, FIRST)])
     other = Blocks(w_down[FIRST:], [(0, 0, 0, rows - FIRST)])
     first_up, first_down = first.sent("x", 1, "first_x_up"), first.sent("x", -1, "first_x_down")
     first_far = first.sent("x", 2, "first_x_far")
     other_z, other_z_last = ring(other, "z", NZ, "other_z")
+    activations, out_grads = (after(a, *[b.array for b in (*other_z[0], first_up, first_down, first_far)]) for a in (activations, out_grads))
+    in_part = jnp.dot(activations, proj_in, preferred_element_type=jnp.float32)
+    in_high = in_part.astype(jnp.bfloat16)
+    in_low = (in_part - in_high.astype(jnp.float32)).astype(jnp.bfloat16)
+    own = jnp.concatenate([out_grads.T, in_high.T, in_low.T], axis=0)
+    own = with_layout_constraint(own, Layout(major_to_minor=(0, 1)))
+
     near = joined([other, *other_z[0], other_z[1][0]])
     far = joined([other_z[1][1], *other_z[2], *other_z_last])
     near = near.after(first_up, first_down, first_far)

time: 182 us -> 190 us (1.044)
  blocking collectives: 21.4 us -> 23.9 us
  waiting for transfers between devices: 60 us -> 62.4 us
    all_to_all x1, blocking collectives: 21.4 us -> 23.9 us  [hand_over(): got = lax.all_to_all(spread, 'dp', split_axis=0, concat_axis=0, tiled=True)]
    ppermute x25, waiting for transfers between devices: 53.9 us -> 56.3 us  [move(): return lax.ppermute(array, 'dp', pairs)]
    optimization_barrier x1 -> x2, local copies, waits for them, and re-layouts: 5.62 us -> 7.15 us  [after(): return lax.optimization_barrier((array, *others))[0]]
  transfers between devices with their start and end apart: 27 -> 27, of which waited for: 15 -> 15; matrix products, arithmetic and copies ran while one was open for 5% -> 6% of each run, Pallas kernels for 7% -> 7%
where the time goes in v4:
time: 190 us; the launch traced here: 189 us
  waiting for transfers between devices  62.4 us (33%)
  starting transfers between devices  43.6 us (23%)
  Pallas kernels  25.2 us (13%)
  blocking collectives  23.9 us (13%)
  between operations  13.7 us (7%)
  local copies, waits for them, and re-layouts  12.7 us (7%)
  other arithmetic  4.82 us (3%)
  matrix products  3.21 us (2%)
    ppermute x25, waiting for transfers between devices, move(): return lax.ppermute(array, 'dp', pairs)  56.3 us
    ppermute x25, starting transfers between devices, move(): return lax.ppermute(array, 'dp', pairs)  38.6 us
    pallas_call x2, Pallas kernels, project(): pl.pallas_call(functools.partial(project_kernel, stretches, start), out_s...  25.2 us
    all_to_all x1, blocking collectives, hand_over(): got = lax.all_to_all(spread, 'dp', split_axis=0, concat_axis=0, tiled=True)  23.9 us
    optimization_barrier x2, local copies, waits for them, and re-layouts, after(): return lax.optimization_barrier((array, *others))[0]  7.15 us
    all_to_all x1, waiting for transfers between devices, shards(): lax.all_to_all(part, 'tensor', split_axis=0, concat_axis=0, tiled=True)  6.05 us
    all_to_all x1, starting transfers between devices, shards(): lax.all_to_all(part, 'tensor', split_axis=0, concat_axis=0, tiled=True)  4.98 us
  transfers between devices with their start and end apart: 27, of which 15 were waited for; matrix products, arithmetic and copies ran while one was open for 6% of the time, Pallas kernels for 7%

profile of v4, /device:TPU:32, one launch (start us, length us, event | category | flops | bytes accessed | tf_op | source)
XLA Modules:
  0.0 189.4 jit_solution(9902943713961069460)
XLA Ops:
  6.5 1.2 fusion.11
  7.7 1.6 collective-permute-start.2
  9.3 1.7 collective-permute-start.3
  11.0 1.8 collective-permute-start.4
  12.8 1.9 %collective-permute-start = (bf16[896,128]{1,0:T(8,128)(2,1)S(1)}, bf16[896,128]{1,0:T(8,128)(2,1)S(1)}, u32[]{:S(2)}, u32[]{:S(2)}) collective-permute-start(bf16[896,128]{1,0:T(8,128)(2,1)S(1)} %get-tuple-element.28), channel_id=1, source_target_pairs={{0,32},{8,40},{16,48},{24,56},{32,64},{40,72},{48,80},{56,88},{64,... | collective-permute-start | bytes 688136 | tf_op jit(solution)/shard_map/other_z_up1/ppermute | solution.py:22
  14.8 0.1 collective-permute-start.1
  14.9 1.6 collective-permute-done.2
  16.5 4.0 %collective-permute-done.3 = bf16[896,128]{1,0:T(8,128)(2,1)S(1)} collective-permute-done((bf16[896,128]{1,0:T(8,128)(2,1)S(1)}, bf16[896,128]{1,0:T(8,128)(2,1)S(1)}, u32[]{:S(2)}, u32[]{:S(2)}) %collective-permute-start.3) | collective-permute-done | bytes 229408 | tf_op jit(solution)/shard_map/first_x_down/ppermute | solution.py:25
  20.5 1.7 collective-permute-done.4
  22.3 0.7 copy-done.3
  22.9 1.5 copy.14
  24.5 0.4 subtract_convert_fusion
  24.9 1.1 pad_maximum_fusion
  26.1 0.0 all-gather.3.cloned.1.call-update
  26.1 2.0 %collective-permute-start.5 = (bf16[896,128]{1,0:T(8,128)(2,1)S(1)}, bf16[896,128]{1,0:T(8,128)(2,1)S(1)}, u32[]{:S(2)}, u32[]{:S(2)}) collective-permute-start(bf16[896,128]{1,0:T(8,128)(2,1)S(1)} %collective-permute-done), channel_id=1, source_target_pairs={{0,32},{8,40},{16,48},{24,56},{32,64},{40,72},{48,80},{56,88},{64,... | collective-permute-start | bytes 688136 | tf_op jit(solution)/shard_map/other_z_up2/ppermute | solution.py:22
  28.1 0.1 collective-permute-start.8
  28.2 1.0 pad_maximum_fusion.1.refs_0_
  29.2 3.4 %collective-permute-done.5 = bf16[896,128]{1,0:T(8,128)(2,1)S(1)} collective-permute-done((bf16[896,128]{1,0:T(8,128)(2,1)S(1)}, bf16[896,128]{1,0:T(8,128)(2,1)S(1)}, u32[]{:S(2)}, u32[]{:S(2)}) %collective-permute-start.5) | collective-permute-done | bytes 229408 | tf_op jit(solution)/shard_map/other_z_up2/ppermute | solution.py:22
  32.6 1.9 %collective-permute-start.6 = (bf16[896,128]{1,0:T(8,128)(2,1)S(1)}, bf16[896,128]{1,0:T(8,128)(2,1)S(1)}, u32[]{:S(2)}, u32[]{:S(2)}) collective-permute-start(bf16[896,128]{1,0:T(8,128)(2,1)S(1)} %collective-permute-done.5), channel_id=1, source_target_pairs={{0,32},{8,40},{16,48},{24,56},{32,64},{40,72},{48,80},{56,88},{64,... | collective-permute-start | bytes 688136 | tf_op jit(solution)/shard_map/other_z_up3/ppermute | solution.py:22
  34.5 2.3 %collective-permute-start.9 = (bf16[896,128]{1,0:T(8,128)(2,1)S(1)}, bf16[896,128]{1,0:T(8,128)(2,1)S(1)}, u32[]{:S(2)}, u32[]{:S(2)}) collective-permute-start(bf16[896,128]{1,0:T(8,128)(2,1)S(1)} %collective-permute-done.8), channel_id=1, source_target_pairs={{0,224},{8,232},{16,240},{24,248},{32,0},{40,8},{48,16},{56,24},{6... | collective-permute-start | bytes 688136 | tf_op jit(solution)/shard_map/other_z_down3/ppermute | solution.py:22
  36.9 0.1 pad_maximum_fusion.2.refs_0_
  36.9 0.9 collective-permute-start.13
  37.9 3.1 %collective-permute-done.6 = bf16[896,128]{1,0:T(8,128)(2,1)S(1)} collective-permute-done((bf16[896,128]{1,0:T(8,128)(2,1)S(1)}, bf16[896,128]{1,0:T(8,128)(2,1)S(1)}, u32[]{:S(2)}, u32[]{:S(2)}) %collective-permute-start.6) | collective-permute-done | bytes 229408 | tf_op jit(solution)/shard_map/other_z_up3/ppermute | solution.py:22
  41.0 0.1 collective-permute-start.7
  41.0 0.5 collective-permute-done.9
  41.6 2.7 %collective-permute-start.10 = (bf16[448,128]{1,0:T(8,128)(2,1)S(1)}, bf16[448,128]{1,0:T(8,128)(2,1)S(1)}, u32[]{:S(2)}, u32[]{:S(2)}) collective-permute-start(bf16[448,128]{1,0:T(8,128)(2,1)S(1)} %slice.40), channel_id=1, source_target_pairs={{0,224},{8,232},{16,240},{24,248},{32,0},{40,8},{48,16},{56,24},{6... | collective-permute-start | bytes 344072 | tf_op jit(solution)/shard_map/other_z_down_last/ppermute | solution.py:22
  44.4 2.6 %collective-permute-done.7 = bf16[448,128]{1,0:T(8,128)(2,1)S(1)} collective-permute-done((bf16[448,128]{1,0:T(8,128)(2,1)S(1)}, bf16[448,128]{1,0:T(8,128)(2,1)S(1)}, u32[]{:S(2)}, u32[]{:S(2)}) %collective-permute-start.7) | collective-permute-done | bytes 114720 | tf_op jit(solution)/shard_map/other_z_up_last/ppermute | solution.py:22
  47.0 0.7 collective-permute-done.10
  47.7 1.8 collective-permute-start.14
  49.4 2.7 %collective-permute-start.12 = (bf16[3584,128]{1,0:T(8,128)(2,1)S(1)}, bf16[3584,128]{1,0:T(8,128)(2,1)S(1)}, u32[]{:S(2)}, u32[]{:S(2)}) collective-permute-start(bf16[3584,128]{1,0:T(8,128)(2,1)S(1)} %pad_maximum_fusion.1.refs_0_), channel_id=1, source_target_pairs={{0,224},{8,232},{16,240},{24,248},{32,0},{40,8},{48,16},{56,24},{6... | collective-permute-start | bytes 2752520 | tf_op jit(solution)/shard_map/first_z_down1/ppermute | solution.py:22
  52.1 1.5 collective-permute-start.11
  53.6 0.4 collective-permute-start.18
  54.0 4.6 %collective-permute-done.13.refs_2_ = bf16[3584,128]{1,0:T(8,128)(2,1)S(1)} collective-permute-done((bf16[3584,128]{1,0:T(8,128)(2,1)S(1)}, bf16[3584,128]{1,0:T(8,128)(2,1)S(1)}, u32[]{:S(2)}, u32[]{:S(2)}) %collective-permute-start.13) | collective-permute-done | bytes 917536 | tf_op jit(solution)/shard_map/other_x_up1_one/ppermute | solution.py:25
  58.5 12.5 %collective-permute-done.14.refs_3_ = bf16[3584,128]{1,0:T(8,128)(2,1)S(1)} collective-permute-done((bf16[3584,128]{1,0:T(8,128)(2,1)S(1)}, bf16[3584,128]{1,0:T(8,128)(2,1)S(1)}, u32[]{:S(2)}, u32[]{:S(2)}) %collective-permute-start.14) | collective-permute-done | bytes 917536 | tf_op jit(solution)/shard_map/other_x_down1_two/ppermute | solution.py:25
  71.1 2.6 %collective-permute-start.16 = (bf16[3584,128]{1,0:T(8,128)(2,1)S(1)}, bf16[3584,128]{1,0:T(8,128)(2,1)}, u32[]{:S(2)}, u32[]{:S(2)}) collective-permute-start(bf16[3584,128]{1,0:T(8,128)(2,1)S(1)} %collective-permute-done.12.refs_2_), channel_id=1, source_target_pairs={{0,224},{8,232},{16,240},{24,248},{32,0},{40,8},{48,16},{56,24},{6... | collective-permute-start | bytes 2752520 | tf_op jit(solution)/shard_map/first_z_down2/ppermute | solution.py:22
  73.7 0.9 collective-permute-start.15
  74.6 11.4 %collective-permute-done.18.refs_5_ = bf16[3584,128]{1,0:T(8,128)(2,1)S(1)} collective-permute-done((bf16[3584,128]{1,0:T(8,128)(2,1)S(1)}, bf16[3584,128]{1,0:T(8,128)(2,1)S(1)}, u32[]{:S(2)}, u32[]{:S(2)}) %collective-permute-start.18) | collective-permute-done | bytes 917536 | tf_op jit(solution)/shard_map/other_x_down1_one/ppermute | solution.py:25
  86.0 3.9 %collective-permute-done.16.refs_4_ = bf16[3584,128]{1,0:T(8,128)(2,1)} collective-permute-done((bf16[3584,128]{1,0:T(8,128)(2,1)S(1)}, bf16[3584,128]{1,0:T(8,128)(2,1)}, u32[]{:S(2)}, u32[]{:S(2)}) %collective-permute-start.16) | collective-permute-done | bytes 917536 | tf_op jit(solution)/shard_map/first_z_down2/ppermute | solution.py:22
  89.9 1.3 collective-permute-start.20
  91.2 0.5 collective-permute-done.15.refs_3_
  91.7 1.3 collective-permute-start.19
  93.1 0.1 select_reduce_fusion
  93.2 2.9 %collective-permute-start.23 = (bf16[3584,128]{1,0:T(8,128)(2,1)}, bf16[3584,128]{1,0:T(8,128)(2,1)}, u32[]{:S(2)}, u32[]{:S(2)}) collective-permute-start(bf16[3584,128]{1,0:T(8,128)(2,1)} %copy-done.8), channel_id=1, source_target_pairs={{0,8},{8,16},{16,24},{24,0},{32,40},{40,48},{48,56},{56,32},{64,72... | collective-permute-start | bytes 2752520 | tf_op jit(solution)/shard_map/other_x_up_last/ppermute | solution.py:25
  96.0 2.4 %collective-permute-start.24 = (bf16[3584,128]{1,0:T(8,128)(2,1)}, bf16[3584,128]{1,0:T(8,128)(2,1)}, u32[]{:S(2)}, u32[]{:S(2)}) collective-permute-start(bf16[3584,128]{1,0:T(8,128)(2,1)} %copy-done.11), channel_id=1, source_target_pairs={{0,24},{8,0},{16,8},{24,16},{32,56},{40,32},{48,40},{56,48},{64,88... | collective-permute-start | bytes 2752520 | tf_op jit(solution)/shard_map/other_x_down_last/ppermute | solution.py:25
  98.5 0.6 pad_add_fusion.place_ref
  99.0 0.1 fusion.9
  99.1 5.6 %copy.15 = bf16[896,1792]{0,1:T(8,128)(2,1)} copy(bf16[896,1792]{1,0:T(8,128)(2,1)} %param.10) | data formatting | bytes 6422528 | tf_op jit(solution)/shard_map/optimization_barrier | solution.py:62
  104.7 5.7 %collective-permute-done.20.refs_6_ = bf16[3584,128]{1,0:T(8,128)(2,1)S(1)} collective-permute-done((bf16[3584,128]{1,0:T(8,128)(2,1)}, bf16[3584,128]{1,0:T(8,128)(2,1)S(1)}, u32[]{:S(2)}, u32[]{:S(2)}) %collective-permute-start.20) | collective-permute-done | bytes 917536 | tf_op jit(solution)/shard_map/first_z_down3/ppermute | solution.py:22
  110.5 1.6 collective-permute-start.22
  112.0 1.0 slice.41
  113.1 2.1 %collective-permute-start.21 = (bf16[1792,128]{1,0:T(8,128)(2,1)S(1)}, bf16[1792,128]{1,0:T(8,128)(2,1)}, u32[]{:S(2)}, u32[]{:S(2)}) collective-permute-start(bf16[1792,128]{1,0:T(8,128)(2,1)S(1)} %slice.41), channel_id=1, source_target_pairs={{0,32},{8,40},{16,48},{24,56},{32,64},{40,72},{48,80},{56,88},{64,... | collective-permute-start | bytes 1376264 | tf_op jit(solution)/shard_map/first_z_up_last/ppermute | solution.py:22
  115.2 1.8 convert_reduce_fusion
  117.1 12.6 %shard_map.83 = f32[64,896]{1,0:T(8,128)} custom-call(s32[4]{0:T(128)} %pad_add_fusion.place_ref, bf16[8,640,896]{2,1,0:T(8,128)(2,1)} %bitcast.28, bf16[1792,896]{1,0:T(8,128)(2,1)} %bitcast.25, bf16[64,1792]{1,0:T(8,128)(2,1)} %bitcast.30, bf16[3584,128]{1,0:T(8,128)(2,1)} %copy-done.2, bf16[3584,128]{1,0:T(8,128)(2,1)} %copy-done.7, ...), custom_call_target="tpu_custom_call" | custom-call | flops 6987710464 | bytes 16285696 | tf_op jit(solution)/shard_map/pallas_call | solution.py:155
  129.7 0.8 copy-done.14
  130.5 12.6 %shard_map.82 = f32[64,896]{1,0:T(8,128)} custom-call(s32[4]{0:T(128)} %pad_add_fusion.place_ref, bf16[8,640,896]{2,1,0:T(8,128)(2,1)} %bitcast.29, bf16[1792,896]{1,0:T(8,128)(2,1)} %bitcast.26, bf16[64,1792]{1,0:T(8,128)(2,1)} %bitcast.31, bf16[3584,128]{1,0:T(8,128)(2,1)} %copy-done.1, bf16[3584,128]{1,0:T(8,128)(2,1)} %copy-done.10, ...), custom_call_target="tpu_custom_call" | custom-call | flops 6987710464 | bytes 16285696 | tf_op jit(solution)/shard_map/pallas_call | solution.py:155
  143.1 2.6 %fusion = f32[8,64,64]{2,1,0:T(8,128)S(1)} fusion(f32[64,896]{1,0:T(8,128)S(1)} %slice_add_fusion, f32[8,896]{1,0:T(8,128)S(1)} %fusion.9, f32[64,896]{1,0:T(8,128)} %shard_map.82, f32[64,896]{1,0:T(8,128)S(1)} %copy-done.5), kind=kOutput, calls=%fused_computation.1 | convolution fusion | flops 352837632 | bytes 847872 | tf_op jit(solution)/shard_map/cpt,qt->cpq/dot_general | solution.py:239
  145.7 0.1 reshape.75
  145.8 0.7 copy.18
  146.6 5.0 %all-to-all-start = ((f32[8,8,512]{2,1,0:T(8,128)}), f32[8,8,512]{2,1,0:T(8,128)S(1)}, u32[]{:S(2)}, u32[]{:S(2)}) async-start(f32[8,8,512]{2,1,0:T(8,128)} %bitcast.23), calls=%async_computation | async-start | bytes 262144 | tf_op jit(solution)/shard_map/all_to_all | solution.py:241
  151.5 0.1 dynamic_slice.3
  151.6 6.1 %all-to-all-done = f32[8,8,512]{2,1,0:T(8,128)S(1)} async-done(((f32[8,8,512]{2,1,0:T(8,128)}), f32[8,8,512]{2,1,0:T(8,128)S(1)}, u32[]{:S(2)}, u32[]{:S(2)}) %all-to-all-start) | async-done | bytes 131104 | tf_op jit(solution)/shard_map/all_to_all | solution.py:241
  157.7 0.2 fusion.2
  157.9 23.9 %all_to_all.14 = bf16[32,8,512]{2,1,0:T(8,128)(2,1)S(1)} all-to-all(bf16[32,8,512]{2,1,0:T(8,128)(2,1)S(1)} %fusion.2), channel_id=1, replica_groups=mesh['dp'=32,'tensor'=8] {'dp'}, dimensions={0} | all-to-all | bytes 524288 | tf_op jit(solution)/shard_map/all_to_all | solution.py:193
  181.9 0.7 reshape.76
  (59 shorter events, 0.4 us)
Async XLA Ops:
  6.5 17.9 %copy-start = (bf16[896,512]{1,0:T(8,128)(2,1)S(1)}, bf16[896,512]{1,0:T(8,128)(2,1)}, u32[]{:S(2)}) copy-start(bf16[896,512]{1,0:T(8,128)(2,1)} %param.8) | copy-start | bytes 2752516
  6.5 17.9 %copy-start.6 = (bf16[512,64]{0,1:T(8,128)(2,1)S(1)}, bf16[512,64]{0,1:T(8,128)(2,1)}, u32[]{:S(2)}) copy-start(bf16[512,64]{0,1:T(8,128)(2,1)} %param.12) | copy-start | bytes 196612
  6.5 108.7 %all-gather.3.cloned.1.call-start = ((), (), s32[]{:S(2)}) async-start(), calls=%async_computation.2 | async-start | bytes 10321920 | tf_op jit(solution)/shard_map/all_gather | solution.py:227
  7.7 8.8 %collective-permute-start.2 = (bf16[896,128]{1,0:T(8,128)(2,1)S(1)}, bf16[896,128]{1,0:T(8,128)(2,1)S(1)}, u32[]{:S(2)}, u32[]{:S(2)}) collective-permute-start(bf16[896,128]{1,0:T(8,128)(2,1)S(1)} %get-tuple-element.27), channel_id=1, source_target_pairs={{0,8},{8,16},{16,24},{24,0},{32,40},{40,48},{48,56},{56,32},{64,72... | collective-permute-start | bytes 688136 | tf_op jit(solution)/shard_map/first_x_up/ppermute | solution.py:25
  9.3 11.3 %collective-permute-start.3 = (bf16[896,128]{1,0:T(8,128)(2,1)S(1)}, bf16[896,128]{1,0:T(8,128)(2,1)S(1)}, u32[]{:S(2)}, u32[]{:S(2)}) collective-permute-start(bf16[896,128]{1,0:T(8,128)(2,1)S(1)} %get-tuple-element.27), channel_id=1, source_target_pairs={{0,24},{8,0},{16,8},{24,16},{32,56},{40,32},{48,40},{56,48},{64,88... | collective-permute-start | bytes 688136 | tf_op jit(solution)/shard_map/first_x_down/ppermute | solution.py:25
  11.0 11.2 %collective-permute-start.4 = (bf16[896,128]{1,0:T(8,128)(2,1)S(1)}, bf16[896,128]{1,0:T(8,128)(2,1)S(1)}, u32[]{:S(2)}, u32[]{:S(2)}) collective-permute-start(bf16[896,128]{1,0:T(8,128)(2,1)S(1)} %get-tuple-element.27), channel_id=1, source_target_pairs={{0,16},{8,24},{16,0},{24,8},{32,48},{40,56},{48,32},{56,40},{64,80... | collective-permute-start | bytes 688136 | tf_op jit(solution)/shard_map/first_x_far/ppermute | solution.py:25
  12.8 9.4 %collective-permute-start = (bf16[896,128]{1,0:T(8,128)(2,1)S(1)}, bf16[896,128]{1,0:T(8,128)(2,1)S(1)}, u32[]{:S(2)}, u32[]{:S(2)}) collective-permute-start(bf16[896,128]{1,0:T(8,128)(2,1)S(1)} %get-tuple-element.28), channel_id=1, source_target_pairs={{0,32},{8,40},{16,48},{24,56},{32,64},{40,72},{48,80},{56,88},{64,... | collective-permute-start | bytes 688136 | tf_op jit(solution)/shard_map/other_z_up1/ppermute | solution.py:22
  14.8 7.5 %collective-permute-start.1 = (bf16[896,128]{1,0:T(8,128)(2,1)S(1)}, bf16[896,128]{1,0:T(8,128)(2,1)S(1)}, u32[]{:S(2)}, u32[]{:S(2)}) collective-permute-start(bf16[896,128]{1,0:T(8,128)(2,1)S(1)} %get-tuple-element.28), channel_id=1, source_target_pairs={{0,224},{8,232},{16,240},{24,248},{32,0},{40,8},{48,16},{56,24},{6... | collective-permute-start | bytes 688136 | tf_op jit(solution)/shard_map/other_z_down1/ppermute | solution.py:22
  22.2 0.7 copy-start.3
  26.1 6.5 %collective-permute-start.5 = (bf16[896,128]{1,0:T(8,128)(2,1)S(1)}, bf16[896,128]{1,0:T(8,128)(2,1)S(1)}, u32[]{:S(2)}, u32[]{:S(2)}) collective-permute-start(bf16[896,128]{1,0:T(8,128)(2,1)S(1)} %collective-permute-done), channel_id=1, source_target_pairs={{0,32},{8,40},{16,48},{24,56},{32,64},{40,72},{48,80},{56,88},{64,... | collective-permute-start | bytes 688136 | tf_op jit(solution)/shard_map/other_z_up2/ppermute | solution.py:22
  28.1 6.5 %collective-permute-start.8 = (bf16[896,128]{1,0:T(8,128)(2,1)S(1)}, bf16[896,128]{1,0:T(8,128)(2,1)S(1)}, u32[]{:S(2)}, u32[]{:S(2)}) collective-permute-start(bf16[896,128]{1,0:T(8,128)(2,1)S(1)} %collective-permute-done.1), channel_id=1, source_target_pairs={{0,224},{8,232},{16,240},{24,248},{32,0},{40,8},{48,16},{56,24},{6... | collective-permute-start | bytes 688136 | tf_op jit(solution)/shard_map/other_z_down2/ppermute | solution.py:22
  29.2 22.9 %copy-start.1 = (bf16[3584,128]{1,0:T(8,128)(2,1)}, bf16[3584,128]{1,0:T(8,128)(2,1)S(1)}, u32[]{:S(2)}) copy-start(bf16[3584,128]{1,0:T(8,128)(2,1)S(1)} %pad_maximum_fusion.1.refs_0_) | copy-start | bytes 2752516
  29.2 63.9 %copy-start.16 = (s32[1,8]{1,0:T(1,128)S(1)}, s32[1,8]{1,0:T(1,128)}, u32[]{:S(2)}) copy-start(s32[1,8]{1,0:T(1,128)} %param.14) | copy-start | bytes 100
  32.6 8.3 %collective-permute-start.6 = (bf16[896,128]{1,0:T(8,128)(2,1)S(1)}, bf16[896,128]{1,0:T(8,128)(2,1)S(1)}, u32[]{:S(2)}, u32[]{:S(2)}) collective-permute-start(bf16[896,128]{1,0:T(8,128)(2,1)S(1)} %collective-permute-done.5), channel_id=1, source_target_pairs={{0,32},{8,40},{16,48},{24,56},{32,64},{40,72},{48,80},{56,88},{64,... | collective-permute-start | bytes 688136 | tf_op jit(solution)/shard_map/other_z_up3/ppermute | solution.py:22
  34.5 7.0 %collective-permute-start.9 = (bf16[896,128]{1,0:T(8,128)(2,1)S(1)}, bf16[896,128]{1,0:T(8,128)(2,1)S(1)}, u32[]{:S(2)}, u32[]{:S(2)}) collective-permute-start(bf16[896,128]{1,0:T(8,128)(2,1)S(1)} %collective-permute-done.8), channel_id=1, source_target_pairs={{0,224},{8,232},{16,240},{24,248},{32,0},{40,8},{48,16},{56,24},{6... | collective-permute-start | bytes 688136 | tf_op jit(solution)/shard_map/other_z_down3/ppermute | solution.py:22
  36.9 67.8 %copy-start.2 = (bf16[3584,128]{1,0:T(8,128)(2,1)}, bf16[3584,128]{1,0:T(8,128)(2,1)S(1)}, u32[]{:S(2)}) copy-start(bf16[3584,128]{1,0:T(8,128)(2,1)S(1)} %pad_maximum_fusion.2.refs_0_) | copy-start | bytes 2752516
  36.9 21.6 %collective-permute-start.13 = (bf16[3584,128]{1,0:T(8,128)(2,1)S(1)}, bf16[3584,128]{1,0:T(8,128)(2,1)S(1)}, u32[]{:S(2)}, u32[]{:S(2)}) collective-permute-start(bf16[3584,128]{1,0:T(8,128)(2,1)S(1)} %pad_maximum_fusion.2.refs_0_), channel_id=1, source_target_pairs={{0,8},{8,16},{16,24},{24,0},{32,40},{40,48},{48,56},{56,32},{64,72... | collective-permute-start | bytes 2752520 | tf_op jit(solution)/shard_map/other_x_up1_one/ppermute | solution.py:25
  41.0 6.0 %collective-permute-start.7 = (bf16[448,128]{1,0:T(8,128)(2,1)S(1)}, bf16[448,128]{1,0:T(8,128)(2,1)S(1)}, u32[]{:S(2)}, u32[]{:S(2)}) collective-permute-start(bf16[448,128]{1,0:T(8,128)(2,1)S(1)} %slice.39), channel_id=1, source_target_pairs={{0,32},{8,40},{16,48},{24,56},{32,64},{40,72},{48,80},{56,88},{64,... | collective-permute-start | bytes 344072 | tf_op jit(solution)/shard_map/other_z_up_last/ppermute | solution.py:22
  41.6 6.1 %collective-permute-start.10 = (bf16[448,128]{1,0:T(8,128)(2,1)S(1)}, bf16[448,128]{1,0:T(8,128)(2,1)S(1)}, u32[]{:S(2)}, u32[]{:S(2)}) collective-permute-start(bf16[448,128]{1,0:T(8,128)(2,1)S(1)} %slice.40), channel_id=1, source_target_pairs={{0,224},{8,232},{16,240},{24,248},{32,0},{40,8},{48,16},{56,24},{6... | collective-permute-start | bytes 344072 | tf_op jit(solution)/shard_map/other_z_down_last/ppermute | solution.py:22
  47.7 38.3 %copy-start.7 = (bf16[3584,128]{1,0:T(8,128)(2,1)}, bf16[3584,128]{1,0:T(8,128)(2,1)S(1)}, u32[]{:S(2)}) copy-start(bf16[3584,128]{1,0:T(8,128)(2,1)S(1)} %constant_dynamic-update-slice_fusion.refs_1_) | copy-start | bytes 2752516
  47.7 23.4 %collective-permute-start.14 = (bf16[3584,128]{1,0:T(8,128)(2,1)S(1)}, bf16[3584,128]{1,0:T(8,128)(2,1)S(1)}, u32[]{:S(2)}, u32[]{:S(2)}) collective-permute-start(bf16[3584,128]{1,0:T(8,128)(2,1)S(1)} %constant_dynamic-update-slice_fusion.refs_1_), channel_id=1, source_target_pairs={{0,24},{8,0},{16,8},{24,16},{32,56},{40,32},{48,40},{56,48},{64,88... | collective-permute-start | bytes 2752520 | tf_op jit(solution)/shard_map/other_x_down1_two/ppermute | solution.py:25
  49.4 21.6 %collective-permute-start.12 = (bf16[3584,128]{1,0:T(8,128)(2,1)S(1)}, bf16[3584,128]{1,0:T(8,128)(2,1)S(1)}, u32[]{:S(2)}, u32[]{:S(2)}) collective-permute-start(bf16[3584,128]{1,0:T(8,128)(2,1)S(1)} %pad_maximum_fusion.1.refs_0_), channel_id=1, source_target_pairs={{0,224},{8,232},{16,240},{24,248},{32,0},{40,8},{48,16},{56,24},{6... | collective-permute-start | bytes 2752520 | tf_op jit(solution)/shard_map/first_z_down1/ppermute | solution.py:22
  52.1 21.6 %collective-permute-start.11 = (bf16[3584,128]{1,0:T(8,128)(2,1)S(1)}, bf16[3584,128]{1,0:T(8,128)(2,1)S(1)}, u32[]{:S(2)}, u32[]{:S(2)}) collective-permute-start(bf16[3584,128]{1,0:T(8,128)(2,1)S(1)} %pad_maximum_fusion.1.refs_0_), channel_id=1, source_target_pairs={{0,32},{8,40},{16,48},{24,56},{32,64},{40,72},{48,80},{56,88},{64,... | collective-permute-start | bytes 2752520 | tf_op jit(solution)/shard_map/first_z_up1/ppermute | solution.py:22
  53.6 32.4 %collective-permute-start.18 = (bf16[3584,128]{1,0:T(8,128)(2,1)S(1)}, bf16[3584,128]{1,0:T(8,128)(2,1)S(1)}, u32[]{:S(2)}, u32[]{:S(2)}) collective-permute-start(bf16[3584,128]{1,0:T(8,128)(2,1)S(1)} %pad_maximum_fusion.2.refs_0_), channel_id=1, source_target_pairs={{0,24},{8,0},{16,8},{24,16},{32,56},{40,32},{48,40},{56,48},{64,88... | collective-permute-start | bytes 2752520 | tf_op jit(solution)/shard_map/other_x_down1_one/ppermute | solution.py:25
  58.5 31.4 %copy-start.8 = (bf16[3584,128]{1,0:T(8,128)(2,1)}, bf16[3584,128]{1,0:T(8,128)(2,1)S(1)}, u32[]{:S(2)}) copy-start(bf16[3584,128]{1,0:T(8,128)(2,1)S(1)} %collective-permute-done.13.refs_2_) | copy-start | bytes 2752516
  58.5 27.5 %collective-permute-start.17 = (bf16[3584,128]{1,0:T(8,128)(2,1)S(1)}, bf16[3584,128]{1,0:T(8,128)(2,1)S(1)}, u32[]{:S(2)}, u32[]{:S(2)}) collective-permute-start(bf16[3584,128]{1,0:T(8,128)(2,1)S(1)} %constant_dynamic-update-slice_fusion.refs_1_), channel_id=1, source_target_pairs={{0,8},{8,16},{16,24},{24,0},{32,40},{40,48},{48,56},{56,32},{64,72... | collective-permute-start | bytes 2752520 | tf_op jit(solution)/shard_map/other_x_up1_two/ppermute | solution.py:25
  71.1 22.0 %copy-start.11 = (bf16[3584,128]{1,0:T(8,128)(2,1)}, bf16[3584,128]{1,0:T(8,128)(2,1)S(1)}, u32[]{:S(2)}) copy-start(bf16[3584,128]{1,0:T(8,128)(2,1)S(1)} %collective-permute-done.14.refs_3_) | copy-start | bytes 2752516
  71.1 20.1 %copy-start.9 = (bf16[3584,128]{1,0:T(8,128)(2,1)}, bf16[3584,128]{1,0:T(8,128)(2,1)S(1)}, u32[]{:S(2)}) copy-start(bf16[3584,128]{1,0:T(8,128)(2,1)S(1)} %collective-permute-done.12.refs_2_) | copy-start | bytes 2752516
  71.1 18.8 %collective-permute-start.16 = (bf16[3584,128]{1,0:T(8,128)(2,1)S(1)}, bf16[3584,128]{1,0:T(8,128)(2,1)}, u32[]{:S(2)}, u32[]{:S(2)}) collective-permute-start(bf16[3584,128]{1,0:T(8,128)(2,1)S(1)} %collective-permute-done.12.refs_2_), channel_id=1, source_target_pairs={{0,224},{8,232},{16,240},{24,248},{32,0},{40,8},{48,16},{56,24},{6... | collective-permute-start | bytes 2752520 | tf_op jit(solution)/shard_map/first_z_down2/ppermute | solution.py:22
  73.7 18.0 %copy-start.10 = (bf16[3584,128]{1,0:T(8,128)(2,1)}, bf16[3584,128]{1,0:T(8,128)(2,1)S(1)}, u32[]{:S(2)}) copy-start(bf16[3584,128]{1,0:T(8,128)(2,1)S(1)} %collective-permute-done.11.refs_1_) | copy-start | bytes 2752516
  73.7 18.0 %collective-permute-start.15 = (bf16[3584,128]{1,0:T(8,128)(2,1)S(1)}, bf16[3584,128]{1,0:T(8,128)(2,1)}, u32[]{:S(2)}, u32[]{:S(2)}) collective-permute-start(bf16[3584,128]{1,0:T(8,128)(2,1)S(1)} %collective-permute-done.11.refs_1_), channel_id=1, source_target_pairs={{0,32},{8,40},{16,48},{24,56},{32,64},{40,72},{48,80},{56,88},{64,... | collective-permute-start | bytes 2752520 | tf_op jit(solution)/shard_map/first_z_up2/ppermute | solution.py:22
  86.0 7.0 %copy-start.12 = (bf16[3584,128]{1,0:T(8,128)(2,1)}, bf16[3584,128]{1,0:T(8,128)(2,1)S(1)}, u32[]{:S(2)}) copy-start(bf16[3584,128]{1,0:T(8,128)(2,1)S(1)} %collective-permute-done.18.refs_5_) | copy-start | bytes 2752516
  86.0 7.0 %copy-start.13 = (bf16[3584,128]{1,0:T(8,128)(2,1)}, bf16[3584,128]{1,0:T(8,128)(2,1)S(1)}, u32[]{:S(2)}) copy-start(bf16[3584,128]{1,0:T(8,128)(2,1)S(1)} %collective-permute-done.17.refs_4_) | copy-start | bytes 2752516
  89.9 20.5 %collective-permute-start.20 = (bf16[3584,128]{1,0:T(8,128)(2,1)}, bf16[3584,128]{1,0:T(8,128)(2,1)S(1)}, u32[]{:S(2)}, u32[]{:S(2)}) collective-permute-start(bf16[3584,128]{1,0:T(8,128)(2,1)} %collective-permute-done.16.refs_4_), channel_id=1, source_target_pairs={{0,224},{8,232},{16,240},{24,248},{32,0},{40,8},{48,16},{56,24},{6... | collective-permute-start | bytes 2752520 | tf_op jit(solution)/shard_map/first_z_down3/ppermute | solution.py:22
  91.7 20.4 %collective-permute-start.19 = (bf16[3584,128]{1,0:T(8,128)(2,1)}, bf16[3584,128]{1,0:T(8,128)(2,1)}, u32[]{:S(2)}, u32[]{:S(2)}) collective-permute-start(bf16[3584,128]{1,0:T(8,128)(2,1)} %collective-permute-done.15.refs_3_), channel_id=1, source_target_pairs={{0,32},{8,40},{16,48},{24,56},{32,64},{40,72},{48,80},{56,88},{64,... | collective-permute-start | bytes 2752520 | tf_op jit(solution)/shard_map/first_z_up3/ppermute | solution.py:22
  93.2 23.9 %collective-permute-start.23 = (bf16[3584,128]{1,0:T(8,128)(2,1)}, bf16[3584,128]{1,0:T(8,128)(2,1)}, u32[]{:S(2)}, u32[]{:S(2)}) collective-permute-start(bf16[3584,128]{1,0:T(8,128)(2,1)} %copy-done.8), channel_id=1, source_target_pairs={{0,8},{8,16},{16,24},{24,0},{32,40},{40,48},{48,56},{56,32},{64,72... | collective-permute-start | bytes 2752520 | tf_op jit(solution)/shard_map/other_x_up_last/ppermute | solution.py:25
  96.0 21.0 %collective-permute-start.24 = (bf16[3584,128]{1,0:T(8,128)(2,1)}, bf16[3584,128]{1,0:T(8,128)(2,1)}, u32[]{:S(2)}, u32[]{:S(2)}) collective-permute-start(bf16[3584,128]{1,0:T(8,128)(2,1)} %copy-done.11), channel_id=1, source_target_pairs={{0,24},{8,0},{16,8},{24,16},{32,56},{40,32},{48,40},{56,48},{64,88... | collective-permute-start | bytes 2752520 | tf_op jit(solution)/shard_map/other_x_down_last/ppermute | solution.py:25
  110.4 6.6 %copy-start.4 = (bf16[3584,128]{1,0:T(8,128)(2,1)}, bf16[3584,128]{1,0:T(8,128)(2,1)S(1)}, u32[]{:S(2)}) copy-start(bf16[3584,128]{1,0:T(8,128)(2,1)S(1)} %collective-permute-done.20.refs_6_) | copy-start | bytes 2752516
  110.5 19.3 %collective-permute-start.22 = (bf16[1792,128]{1,0:T(8,128)(2,1)S(1)}, bf16[1792,128]{1,0:T(8,128)(2,1)S(1)}, u32[]{:S(2)}, u32[]{:S(2)}) collective-permute-start(bf16[1792,128]{1,0:T(8,128)(2,1)S(1)} %slice.42), channel_id=1, source_target_pairs={{0,224},{8,232},{16,240},{24,248},{32,0},{40,8},{48,16},{56,24},{6... | collective-permute-start | bytes 1376264 | tf_op jit(solution)/shard_map/first_z_down_last/ppermute | solution.py:22
  113.1 16.6 %collective-permute-start.21 = (bf16[1792,128]{1,0:T(8,128)(2,1)S(1)}, bf16[1792,128]{1,0:T(8,128)(2,1)}, u32[]{:S(2)}, u32[]{:S(2)}) collective-permute-start(bf16[1792,128]{1,0:T(8,128)(2,1)S(1)} %slice.41), channel_id=1, source_target_pairs={{0,32},{8,40},{16,48},{24,56},{32,64},{40,72},{48,80},{56,88},{64,... | collective-permute-start | bytes 1376264 | tf_op jit(solution)/shard_map/first_z_up_last/ppermute | solution.py:22
  129.7 13.4 %copy-start.5 = (f32[64,896]{1,0:T(8,128)S(1)}, f32[64,896]{1,0:T(8,128)}, u32[]{:S(2)}) copy-start(f32[64,896]{1,0:T(8,128)} %shard_map.83) | copy-start | bytes 688132
  129.7 0.8 copy-start.14
  143.1 8.4 %copy-start.15 = (s32[256]{0:T(256)S(1)}, s32[256]{0:T(256)}, u32[]{:S(2)}) copy-start(s32[256]{0:T(256)} %param.15) | copy-start | bytes 3076
  146.6 11.1 %all-to-all-start = ((f32[8,8,512]{2,1,0:T(8,128)}), f32[8,8,512]{2,1,0:T(8,128)S(1)}, u32[]{:S(2)}, u32[]{:S(2)}) async-start(f32[8,8,512]{2,1,0:T(8,128)} %bitcast.23), calls=%async_computation | async-start | bytes 262144 | tf_op jit(solution)/shard_map/all_to_all | solution.py:241
Sparse Core Ops, SparseCore 0:
  26.2 57.1 all-gather.2
